TPU v7x, 256 devices: a whole 4x4x8 slice. The times are simulated.
256 devices in a mesh: rng: 32 (over x, y, core), dop: 8 (over z).
Axes of the slice: x: 4, y: 4, z: 8, core: 2. Of those that a mesh axis runs over, the one named last changes fastest.
Arguments:
- pulses: bfloat16 [2, 512, 256, 4096], P(None, None, 'dop', 'rng'), may hold values from -60 to 60
- guard: int32 [4096], P('rng'), may hold values 0 or 1
- steer_index: int32 [256], P('dop'), may hold values from 0 to 63
Outputs:
- beams: float32 [256, 2, 4096], P('dop', None, 'rng')
All inputs are finite; a program needn't handle non-finite values. No bound on the sum of `guard` on one device may be relied on, other than what follows from the above.
Results may differ from a plain program's by a relative error of at most 0.003.
The roundings to bfloat16 on the way count: a program that leaves them out, or rounds other values in their place, can miss the bound.
Values may be sent and summed in bfloat16 or wider, within the bound.
No kernel may reach another device: no remote copies, remote signals or barrier semaphores. Data moves between devices by JAX's collectives and lax.ppermute only.
A program may use at most 128 MiB of HBM per device.

v0:
```python
import math

import jax
import jax.numpy as jnp
from jax import lax
from jax.sharding import PartitionSpec as P

NANG = 64


LOADING = 0.1


def doppler_table(period, bins):
    pulse_index = jnp.arange(period, dtype=jnp.int32)
    bin_index = jnp.arange(bins, dtype=jnp.int32)
    turn_count = pulse_index[:, None] * bin_index[None, :] % period
    phase_angle = 2.0 * math.pi / period * turn_count.astype(jnp.float32)
    window_taper = 0.54 - 0.46 * jnp.cos(
        2.0 * math.pi / (period - 1) * pulse_index.astype(jnp.float32)
    )
    cosine = window_taper[:, None] * jnp.cos(phase_angle)
    sine_part = window_taper[:, None] * jnp.sin(phase_angle)
    return jnp.stack([jnp.stack([cosine, sine_part]), jnp.stack([-sine_part, cosine])]).astype(
        jnp.bfloat16
    )


def steering(indices, channels):
    sine_of = -0.9 + 1.8 * indices.astype(jnp.float32) / (NANG - 1)
    phase_angle = math.pi * jnp.arange(channels, dtype=jnp.float32)[None, :] * sine_of[:, None]
    return jnp.concatenate([jnp.cos(phase_angle), jnp.sin(phase_angle)], 1)


def covariance(snapshot, weight_rows):
    real_rows = snapshot[:, 0]
    imag_rows = snapshot[:, 1]
    stacked = jnp.concatenate([real_rows, imag_rows], 2)
    turned = jnp.concatenate([imag_rows, -real_rows], 2)
    masking = jnp.concatenate([weight_rows, weight_rows], 1)[:, None, :]
    left_side = jnp.stack([stacked * masking, turned * masking], 1)
    return jnp.einsum("bkir,bjr->bkij", left_side, stacked, preferred_element_type=jnp.float32)


def solve_weights(covariance_sum, steer_vectors, total_cells):
    channels = covariance_sum.shape[-1]
    real_block = covariance_sum[:, 0] / total_cells
    imag_block = covariance_sum[:, 1] / total_cells
    loading = LOADING * jnp.trace(real_block, axis1=1, axis2=2) / channels + 1e-05
    loaded = real_block + loading[:, None, None] * jnp.eye(channels, dtype=jnp.float32)
    full_matrix = jnp.concatenate(
        [jnp.concatenate([loaded, -imag_block], 2), jnp.concatenate([imag_block, loaded], 2)], 1
    )
    lower = jnp.linalg.cholesky(full_matrix)
    first = lax.linalg.triangular_solve(
        lower, steer_vectors[:, :, None], left_side=True, lower=True
    )
    weights = lax.linalg.triangular_solve(
        lower, first, left_side=True, lower=True, transpose_a=True
    )[:, :, 0]
    return (weights.astype(jnp.bfloat16), full_matrix, loading)


def beamform(weights, snapshot):
    channels = snapshot.shape[2]
    real_w = weights[:, :channels]
    imag_w = weights[:, channels:]
    paired = jnp.stack([jnp.stack([real_w, imag_w], 1), jnp.stack([-imag_w, real_w], 1)], 1)
    return jnp.einsum("bokc,bkcr->bor", paired, snapshot, preferred_element_type=jnp.float32)


def train_power(raw_beams, weight_rows):
    return jnp.sum(weight_rows.astype(jnp.float32)[:, None, :] * raw_beams * raw_beams, axis=(1, 2))


def on_device(pulses, guard, steer_index):
    ranks = lax.axis_size("rng")
    bin_dev = steer_index.shape[0]
    owned = bin_dev // ranks
    table = doppler_table(pulses.shape[1], bin_dev * lax.axis_size("dop"))
    spectrum = jnp.einsum(
        "kjpb,jpcr->bkcr", table, pulses, preferred_element_type=jnp.float32
    ).astype(jnp.bfloat16)
    snapshot = lax.all_to_all(spectrum, "dop", split_axis=0, concat_axis=2, tiled=True)
    cell_dev = snapshot.shape[3]
    total_cells = cell_dev * ranks
    training = (1 - guard).astype(jnp.bfloat16)
    first_bin = lax.axis_index("rng") * owned
    steer_vectors = steering(
        lax.dynamic_slice_in_dim(steer_index, first_bin, owned), snapshot.shape[2]
    )
    rows_mask = jnp.broadcast_to(training, (bin_dev, cell_dev))
    covariance_sum = lax.psum_scatter(
        covariance(snapshot, rows_mask), "rng", scatter_dimension=0, tiled=True
    )
    weights, full_matrix, loading = solve_weights(covariance_sum, steer_vectors, total_cells)
    all_weights, all_loading = (
        lax.all_gather(weights.astype(jnp.float32), "rng", axis=0, tiled=True),
        lax.all_gather(loading, "rng", axis=0, tiled=True),
    )
    raw_beams = beamform(all_weights.astype(jnp.bfloat16), snapshot)
    summed = lax.psum(train_power(raw_beams, rows_mask), "rng")
    all_power = summed / total_cells + all_loading * jnp.sum(jnp.square(all_weights), 1)
    return raw_beams * lax.rsqrt(all_power)[:, None, None]


def solution(mesh):
    return jax.shard_map(
        on_device,
        mesh=mesh,
        in_specs=(P(None, None, "dop", "rng"), P("rng"), P("dop")),
        out_specs=P("dop", None, "rng"),
        check_vma=False,
    )
```

profile of v0, /device:TPU:1, one launch (start us, length us, event | category | flops | bytes accessed | tf_op | source)
XLA Modules:
  0.0 503.4 jit_solution(16407631557615189841)
XLA Ops:
  6.6 2.3 fusion.43
  8.9 9.6 %fusion.5 = bf16[256,2,32,128]{3,0,2,1:T(8,128)(2,1)S(1)} fusion(bf16[2,512,32,128]{3,2,1,0:T(8,128)(2,1)} %param.3, bf16[1,2,512,256]{2,3,1,0:T(8,128)(2,1)S(1)} %get-tuple-element.35, bf16[1,2,512,256]{2,3,1,0:T(8,128)(2,1)S(1)} %get-tuple-element.34), kind=kOutput, calls=%fused_computation.9 | convolution fusion | flops 4299161600 | bytes 13631488 | tf_op jit(solution)/shard_map/kjpb,jpcr->bkcr/dot_general | solution.py:81
  18.6 4.7 copy.34
  23.2 9.1 %all-to-all-start = ((bf16[256,2,32,128]{3,2,1,0:T(8,128)(2,1)}), bf16[256,2,32,128]{3,2,1,0:T(8,128)(2,1)}, u32[]{:S(2)}, u32[]{:S(2)}) async-start(bf16[256,2,32,128]{3,2,1,0:T(8,128)(2,1)} %copy.34), calls=%async_computation | async-start | bytes 8388608 | tf_op jit(solution)/shard_map/all_to_all | solution.py:84
  32.5 96.8 %all-to-all-done = bf16[256,2,32,128]{3,2,1,0:T(8,128)(2,1)} async-done(((bf16[256,2,32,128]{3,2,1,0:T(8,128)(2,1)}), bf16[256,2,32,128]{3,2,1,0:T(8,128)(2,1)}, u32[]{:S(2)}, u32[]{:S(2)}) %all-to-all-start) | async-done | bytes 4194336 | tf_op jit(solution)/shard_map/all_to_all | solution.py:84
  129.2 3.3 copy.35
  132.6 3.2 slice_bitcast_fusion.43
  135.8 2.1 maximum_multiply_fusion
  137.8 9.0 %fusion.2 = f32[32,2,256,256]{2,3,1,0:T(8,128)} fusion(bf16[32,256,128]{2,1,0:T(8,128)(2,1)} %get-tuple-element.27, bf16[32,256,128]{2,1,0:T(8,128)(2,1)} %get-tuple-element.25, bf16[32,1,256,256]{3,2,0,1:T(8,128)(2,1)S(1)} %get-tuple-element.31, bf16[32,1,256,256]{3,2,0,1:T(8,128)(2,1)S(1)} %get-tuple-element.30), kind=kOutput, calls=%fused_computation.6 | convolution fusion | flops 2160066560 | bytes 29360128 | tf_op jit(solution)/shard_map/bkir,bjr->bkij/dot_general | solution.py:42
  146.9 0.6 copy-done.2
  147.5 0.6 dynamic_slice.3
  148.8 0.6 dynamic-slice.4
  149.5 115.0 %reduce-scatter.2.cloned.1.call-done = f32[1,2,256,256]{2,3,1,0:T(8,128)} async-done(((f32[32,2,256,256]{2,3,1,0:T(8,128)}), f32[1,2,256,256]{2,3,1,0:T(8,128)}) %reduce-scatter.2.cloned.1.call-update) | async-done | bytes 524304 | tf_op jit(solution)/shard_map/reduce_scatter | solution.py:93
  264.6 1.7 fusion.45
  266.9 1.0 fusion.44
  267.9 1.1 fusion.83
  269.1 0.3 copy.38
  269.4 0.2 fusion.36
  269.6 11.7 %custom-call.36 = f32[1,128,128]{2,1,0:T(8,128)S(1)} custom-call(f32[1,128,128]{2,1,0:T(8,128)S(1)} %cholesky.267), custom_call_target="Cholesky" | custom-call | tf_op jit(solution)/shard_map/jit(cholesky)/cholesky | solution.py:54
  281.5 9.8 %custom-call.37 = f32[1,1,128,128]{2,3,1,0:T(8,128)S(1)} custom-call(f32[1,1,128,128]{3,2,1,0:T(8,128)S(1)} %get-tuple-element.45), custom_call_target="InvertDiagBlocksLowerTriangular" | custom-call | tf_op jit(solution)/shard_map/jit(cholesky)/cholesky | solution.py:54
  291.3 0.3 constant_dynamic-update-slice_fusion.3
  291.6 0.3 fusion.12
  292.0 11.7 %custom-call.38 = f32[1,128,128]{2,1,0:T(8,128)S(1)} custom-call(f32[1,128,128]{2,1,0:T(8,128)S(1)} %cholesky.271), custom_call_target="Cholesky" | custom-call | tf_op jit(solution)/shard_map/jit(cholesky)/cholesky | solution.py:54
  303.7 10.0 %custom-call.39 = f32[1,1,128,128]{2,3,1,0:T(8,128)S(1)} custom-call(f32[1,1,128,128]{3,2,1,0:T(8,128)S(1)} %get-tuple-element.42), custom_call_target="InvertDiagBlocksLowerTriangular" | custom-call | tf_op jit(solution)/shard_map/jit(cholesky)/cholesky | solution.py:54
  313.7 0.3 fusion.13
  314.0 0.4 fusion.14
  314.4 11.7 %custom-call.40 = f32[1,128,128]{2,1,0:T(8,128)S(1)} custom-call(f32[1,128,128]{2,1,0:T(8,128)S(1)} %cholesky.276), custom_call_target="Cholesky" | custom-call | tf_op jit(solution)/shard_map/jit(cholesky)/cholesky | solution.py:54
  326.1 9.8 %custom-call.41 = f32[1,1,128,128]{2,3,1,0:T(8,128)S(1)} custom-call(f32[1,1,128,128]{3,2,1,0:T(8,128)S(1)} %get-tuple-element.39), custom_call_target="InvertDiagBlocksLowerTriangular" | custom-call | tf_op jit(solution)/shard_map/jit(cholesky)/cholesky | solution.py:54
  335.9 0.2 fusion.15
  336.1 0.4 fusion.16
  336.5 11.7 %custom-call.42 = f32[1,128,128]{2,1,0:T(8,128)S(1)} custom-call(f32[1,128,128]{2,1,0:T(8,128)S(1)} %fusion.16), custom_call_target="Cholesky" | custom-call | tf_op jit(solution)/shard_map/jit(cholesky)/cholesky | solution.py:54
  348.2 0.2 select_reduce_fusion
  348.5 0.7 compare_reduce_fusion.1
  349.2 0.6 compare_reduce_fusion
  349.8 0.7 compare_reduce_fusion.2
  353.1 7.9 %while.1 = (s32[]{:T(128)}, f32[1,512,512]{2,1,0:T(8,128)S(1)}, s32[4,2]{0,1:T(2,128)S(1)}, f32[4,1,128,128]{3,2,1,0:T(8,128)S(1)}, s32[]{:T(128)}) while((s32[]{:T(128)}, f32[1,512,512]{2,1,0:T(8,128)S(1)}, s32[4,2]{0,1:T(2,128)S(1)}, f32[4,1,128,128]{3,2,1,0:T(8,128)S(1)}, s32[]{:T(128)}) %tuple.45), condition=%wide.while_cond, body=%wide.while_body.sunk | while | flops 2 | bytes 131189 | solution.py:58
  353.2 0.6 fusion.96
  353.8 1.3 bitcast_dynamic-update-slice_fusion.2
  355.2 0.6 fusion.96
  355.7 1.3 bitcast_dynamic-update-slice_fusion.2
  357.1 0.6 fusion.96
  357.7 1.3 bitcast_dynamic-update-slice_fusion.2
  359.1 0.6 fusion.96
  359.7 1.3 bitcast_dynamic-update-slice_fusion.2
  361.0 39.3 %custom-call.43 = f32[1,4,128,128]{2,3,1,0:T(8,128)S(1)} custom-call(f32[1,4,128,128]{3,2,1,0:T(8,128)S(1)} %bitcast.323), custom_call_target="InvertDiagBlocksLowerTriangular" | custom-call | tf_op jit(solution)/shard_map/triangular_solve | solution.py:58
  400.5 0.2 fusion.25
  400.7 0.2 fusion.54
  400.9 0.2 fusion.26
  401.1 0.2 fusion.55
  401.3 0.3 fusion.33
  401.6 0.2 convolution_bitcast_fusion.10
  401.8 0.2 bitcast_convert_fusion.1
  402.0 0.2 fusion.22
  402.2 0.2 fusion.85
  402.4 0.2 fusion.27
  402.6 0.2 fusion.86
  402.8 0.3 fusion.31
  403.0 0.2 fusion.29
  403.3 25.8 %all-gather = f32[32,512,1]{1,2,0:T(1,128)S(1)} all-gather(f32[1,512,1]{1,2,0:T(1,128)S(1)} %maximum_convert_fusion), channel_id=2, replica_groups=mesh['rng'=32,'dop'=8] {'rng'}, dimensions={0}, use_global_device_ids=true | all-gather | bytes 67584 | tf_op jit(solution)/shard_map/all_gather | solution.py:98
  429.1 0.3 multiply_reduce_fusion
  429.5 3.1 fusion.57
  432.7 0.7 dynamic-update-slice.23
  433.4 62.2 %all-reduce.2 = (f32[32]{0:T(128)S(1)}, f32[32]{0:T(128)S(1)}) all-reduce(f32[32]{0:T(128)S(1)} %dynamic-update-slice.23, f32[32]{0:T(128)S(1)} %get-tuple-element.64), channel_id=1, replica_groups=mesh['rng'=32,'dop'=8] {'rng'}, use_global_device_ids=true, to_apply=%add.1 | all-reduce | flops 64 | bytes 512
  495.6 0.7 broadcast_multiply_fusion
  (41 shorter events, 1.4 us)
Async XLA Ops:
  23.2 9.2 %copy-start.1 = (s32[128]{0:T(128)S(1)}, s32[128]{0:T(128)}, u32[]{:S(2)}) copy-start(s32[128]{0:T(128)} %param.4) | copy-start | bytes 1540
  23.2 106.0 %all-to-all-start = ((bf16[256,2,32,128]{3,2,1,0:T(8,128)(2,1)}), bf16[256,2,32,128]{3,2,1,0:T(8,128)(2,1)}, u32[]{:S(2)}, u32[]{:S(2)}) async-start(bf16[256,2,32,128]{3,2,1,0:T(8,128)(2,1)} %copy.34), calls=%async_computation | async-start | bytes 8388608 | tf_op jit(solution)/shard_map/all_to_all | solution.py:84
  32.4 232.2 %reduce-scatter.2.cloned.1.call-start = ((), (), s32[]{:S(2)}) async-start(), calls=%async_computation.2 | async-start | bytes 17301504 | tf_op jit(solution)/shard_map/reduce_scatter | solution.py:93
  132.6 3.2 copy-start
  146.9 0.7 copy-start.2
  146.9 1.9 copy-start.3
Sparse Core Ops, SparseCore 0:
  147.0 117.4 reduce-scatter.1
where the time goes:
time: 513 us; the launch traced here: 503 us
  waiting for transfers between devices  212 us (41%)
  other arithmetic  131 us (26%)
  blocking collectives  88 us (17%)
  matrix products  26.5 us (5%)
  local copies, waits for them, and re-layouts  19 us (4%)
  between operations  17.8 us (3%)
  starting transfers between devices  9.18 us (2%)
    reduce_scatter x1, waiting for transfers between devices, on_device(): lax.psum_scatter(covariance(snapshot, rows_mask), 'rng', scatter_dimensio...  115 us
    all_to_all x1, waiting for transfers between devices, on_device(): lax.all_to_all(spectrum, 'dop', split_axis=0, concat_axis=2, tiled=True)  96.8 us
    another operation x14, other arithmetic, solve_weights(): lower = jnp.linalg.cholesky(full_matrix)  78.8 us
    unnamed x1, blocking collectives  62.2 us
    another operation x3, other arithmetic, solve_weights(): lax.linalg.triangular_solve(lower, first, left_side=True, lower=True, tra...  39.4 us
    all_gather x1, blocking collectives, on_device(): lax.all_gather(weights.astype(jnp.float32), 'rng', axis=0, tiled=True)  25.8 us
  transfers between devices with their start and end apart: 2, of which 2 were waited for; matrix products, arithmetic and copies ran while one was open for 0% of the time, Pallas kernels for 0%

commit v1 on v0

v1 whole, which is shorter than its diff:
```python
import functools, math
import jax, jax.numpy as jnp
from jax import lax
from jax.experimental import pallas as pl
from jax.experimental.pallas import tpu as pltpu
HI = lax.Precision.HIGHEST
CELLS=4096
NB=32

def lane(x, j):
    return jnp.broadcast_to(x[:, j:j+1], x.shape)
def sub(x, j):
    return jnp.broadcast_to(x[j:j+1, :], x.shape)

def gj1(ar, ai, n):
    row = lax.broadcasted_iota(jnp.int32, (8,128), 0)
    for j in range(n):
        g, jj = divmod(j, 8)
        rr, ri = sub(ar[g], jj), sub(ai[g], jj)
        t = 1.0 / lane(rr, j)
        nr, ni = rr * t, ri * t
        br, bi = [], []
        for h in range(n // 8):
            cr, ci = lane(ar[h], j), lane(ai[h], j)
            ur = ar[h] - (cr * nr - ci * ni)
            ui = ai[h] - (cr * ni + ci * nr)
            if h == g:
                ur = jnp.where(row == jj, nr, ur); ui = jnp.where(row == jj, ni, ui)
            br.append(ur); bi.append(ui)
        ar, ai = br, bi
    return ar, ai

def gj2(ar, ai, n):
    row = lax.broadcasted_iota(jnp.int32, (8,128), 0)
    for j in range(0, n, 2):
        g, jj = divmod(j, 8)
        pr, pi = sub(ar[g], jj), sub(ai[g], jj)
        qr, qi = sub(ar[g], jj+1), sub(ai[g], jj+1)
        a, d = lane(pr, j), lane(qr, j+1)
        b, e = lane(pr, j+1), lane(pi, j+1)
        t = 1.0 / (a * d - (b * b + e * e))
        npr = (d * pr - (b * qr - e * qi)) * t
        npi = (d * pi - (b * qi + e * qr)) * t
        nqr = (a * qr - (b * pr + e * pi)) * t
        nqi = (a * qi - (b * pi - e * pr)) * t
        br, bi = [], []
        for h in range(n // 8):
            cr, ci = lane(ar[h], j), lane(ai[h], j)
            dr, di = lane(ar[h], j+1), lane(ai[h], j+1)
            ur = ar[h] - ((cr * npr - ci * npi) + (dr * nqr - di * nqi))
            ui = ai[h] - ((cr * npi + ci * npr) + (dr * nqi + di * nqr))
            if h == g:
                ur = jnp.where(row == jj, npr, jnp.where(row == jj+1, nqr, ur))
                ui = jnp.where(row == jj, npi, jnp.where(row == jj+1, nqi, ui))
            br.append(ur); bi.append(ui)
        ar, ai = br, bi
    return ar, ai

def times_i(x, ch):
    tail = x[:, 2*ch:]
    lane_no = lax.broadcasted_iota(jnp.int32, tail.shape, 1)
    back, fwd = pltpu.roll(tail, 127, 1), pltpu.roll(tail, 1, 1)
    return jnp.concatenate([-x[:, ch:2*ch], x[:, :ch], jnp.where(lane_no == 0, -back, fwd)], 1)

def solve_in(w_ref, ch, gj, prec=HI):
    nb = NB
    n8 = nb // 8
    lanes = lax.broadcasted_iota(jnp.int32, (8,128), 1)
    rows = lax.broadcasted_iota(jnp.int32, (8,128), 0)
    def block(k, _):
        at = pl.ds(pl.multiple_of(k * nb, nb), nb)
        x = w_ref[at, :]
        ar, ai = [], []
        for h in range(n8):
            ar.append(jnp.where(lanes < nb, x[8*h:8*h+8, :128], jnp.where(lanes == nb + 8*h + rows, 1.0, 0.0)))
            ai.append(jnp.where(lanes < nb, x[8*h:8*h+8, ch:ch+128], 0.0))
        ar, ai = gj(ar, ai, nb)
        ar, ai = jnp.concatenate(ar, 0), jnp.concatenate(ai, 0)
        lhs = jnp.concatenate([ar[:, nb:2*nb], ai[:, nb:2*nb]], 1)
        y = jnp.dot(lhs, jnp.concatenate([x, times_i(x, ch)], 0), precision=prec, preferred_element_type=jnp.float32)
        yy = jnp.concatenate([y, times_i(y, ch)], 0)
        c = jnp.concatenate([w_ref[:, :nb], w_ref[:, ch:ch+nb]], 1)
        upd = w_ref[...] - jnp.dot(c, yy, precision=prec, preferred_element_type=jnp.float32)
        w_ref[...] = upd
        w_ref[at, :] = y
        w_ref[:, :ch] = pltpu.roll(w_ref[:, :ch], ch - nb, 1)
        w_ref[:, ch:2*ch] = pltpu.roll(w_ref[:, ch:2*ch], ch - nb, 1)
        return 0
    lax.fori_loop(0, ch // nb, block, 0)

def cov_kernel(x_ref, m_ref, rhs_ref, w_ref, ld_ref, acc_ref):
    ch = 256
    acc_ref[...] = jnp.zeros_like(acc_ref)
    def step(s, _):
        x = x_ref[:, pl.ds(s, 1)].reshape(8, 64, 128)
        m = jnp.broadcast_to(m_ref[pl.ds(s, 1), :].astype(jnp.bfloat16), (ch, 128))
        xr = x[:, :32].reshape(ch, 128) * m
        xi = x[:, 32:].reshape(ch, 128) * m
        a = jnp.concatenate([xr, xi], 1)
        b = jnp.concatenate([xi, -xr], 1)
        acc_ref[...] += lax.dot_general(jnp.concatenate([a, b], 0), a, (((1,), (1,)), ((), ())), preferred_element_type=jnp.float32)
        return 0
    lax.fori_loop(0, 32, step, 0)
    re = acc_ref[:ch] * (1.0 / CELLS)
    im = acc_ref[ch:] * (1.0 / CELLS)
    diag = lax.broadcasted_iota(jnp.int32, (ch, ch), 0) == lax.broadcasted_iota(jnp.int32, (ch, ch), 1)
    ld = 0.1 * jnp.sum(jnp.where(diag, re, 0.0), keepdims=True) / ch + 1e-5
    w_ref[:, :ch] = re + jnp.where(diag, ld, 0.0)
    w_ref[:, ch:2*ch] = im
    w_ref[:, 2*ch:] = rhs_ref[...]
    ld_ref[...] = jnp.broadcast_to(ld, ld_ref.shape)

def beam_part(x_ref, m_ref, w_ref, ld, out_ref):
    ch = 256
    wt = jnp.transpose(w_ref[:, 2*ch:])[:8]
    wt = wt.astype(jnp.bfloat16).astype(jnp.float32)
    wr, wi = wt[0:1], wt[1:2]
    first = lax.broadcasted_iota(jnp.int32, (8, ch), 0)
    lr = jnp.where(first == 0, wr, jnp.where(first == 1, -wi, 0.0)).astype(jnp.bfloat16)
    li = jnp.where(first == 0, wi, jnp.where(first == 1, wr, 0.0)).astype(jnp.bfloat16)
    lhs = jnp.concatenate([lr, li], 1)
    def step(s, p):
        x = x_ref[:, pl.ds(s, 1)].reshape(8, 64, 128)
        x2 = jnp.concatenate([x[:, :32].reshape(ch, 128), x[:, 32:].reshape(ch, 128)], 0)
        raw = jnp.dot(lhs, x2, preferred_element_type=jnp.float32)
        out_ref[pl.ds(s, 1)] = raw[:2].reshape(1, 2, 128)
        return p + raw * raw * m_ref[pl.ds(s, 1), :]
    p = lax.fori_loop(0, 32, step, jnp.zeros((8, 128), jnp.float32))
    sq = jnp.sum(jnp.where(first < 2, wt * wt, 0.0), keepdims=True)
    power = jnp.sum(p, keepdims=True) * (1.0 / CELLS) + ld * sq
    out_ref[...] = out_ref[...] * lax.rsqrt(power).reshape(1, 1, 1)

def full_kernel(gj, parts, x_ref, m_ref, rhs_ref, out_ref, w_ref, acc_ref, ld_ref):
    if "c" in parts: cov_kernel(x_ref, m_ref, rhs_ref, w_ref, ld_ref, acc_ref)
    else:
        w_ref[...] = jnp.zeros_like(w_ref)
        d = lax.broadcasted_iota(jnp.int32, (256, 256), 0) == lax.broadcasted_iota(jnp.int32, (256, 256), 1)
        w_ref[:, :256] = jnp.where(d, 2.0, 0.1)
        w_ref[:, 512:] = rhs_ref[...]
        ld_ref[...] = jnp.ones_like(ld_ref)
    if "s" in parts: solve_in(w_ref, 256, gj)
    if "b" in parts: beam_part(x_ref, m_ref, w_ref, ld_ref[:1, :1], out_ref)
    else: out_ref[...] = w_ref[:64, 512:].reshape(32, 2, 128)

def full(x, m, rhs, gj=gj1, parts="csb", interpret=False):
    return pl.pallas_call(
        functools.partial(full_kernel, gj, parts),
        out_shape=jax.ShapeDtypeStruct((32, 2, 128), jnp.float32),
        in_specs=[pl.BlockSpec(memory_space=pltpu.VMEM)] * 3,
        out_specs=pl.BlockSpec(memory_space=pltpu.VMEM),
        scratch_shapes=[pltpu.VMEM((256, 640), jnp.float32), pltpu.VMEM((512, 256), jnp.float32), pltpu.VMEM((8, 128), jnp.float32)],
        compiler_params=pltpu.CompilerParams(vmem_limit_bytes=40 * 2**20),
        name="solve", interpret=interpret,
    )(x, m, rhs)


from jax.sharding import PartitionSpec as P

NANG = 64


def doppler_table(period, bins):
    pulse_index = jnp.arange(period, dtype=jnp.int32)
    bin_index = jnp.arange(bins, dtype=jnp.int32)
    turn_count = pulse_index[:, None] * bin_index[None, :] % period
    phase_angle = 2.0 * math.pi / period * turn_count.astype(jnp.float32)
    window_taper = 0.54 - 0.46 * jnp.cos(
        2.0 * math.pi / (period - 1) * pulse_index.astype(jnp.float32)
    )
    cosine = window_taper[:, None] * jnp.cos(phase_angle)
    sine_part = window_taper[:, None] * jnp.sin(phase_angle)
    return jnp.stack([jnp.stack([cosine, sine_part]), jnp.stack([-sine_part, cosine])]).astype(
        jnp.bfloat16
    )


def steering(index, channels):
    sine_of = -0.9 + 1.8 * index.astype(jnp.float32) / (NANG - 1)
    phase_angle = math.pi * jnp.arange(channels, dtype=jnp.float32) * sine_of
    pair = jnp.stack([jnp.cos(phase_angle), jnp.sin(phase_angle)], 1)
    return jnp.pad(pair, ((0, 0), (0, 126)))


def on_device(pulses, guard, steer_index):
    bins = steer_index.shape[0] * lax.axis_size("dop")
    table = doppler_table(pulses.shape[1], bins)
    spectrum = jnp.einsum(
        "kjpb,jpcr->bkcr", table, pulses, preferred_element_type=jnp.float32
    ).astype(jnp.bfloat16)
    mask = 1.0 - lax.all_gather(guard, "rng", axis=0).astype(jnp.float32)
    rhs = steering(steer_index[lax.axis_index("rng")], 256)
    snapshot = lax.all_to_all(spectrum, ("dop", "rng"), split_axis=0, concat_axis=0, tiled=True)
    beams = full(snapshot.reshape(8, 32, 64, 128), mask, rhs, gj2)
    return lax.all_to_all(beams, "rng", split_axis=0, concat_axis=0, tiled=True)


def solution(mesh):
    return jax.shard_map(
        on_device,
        mesh=mesh,
        in_specs=(P(None, None, "dop", "rng"), P("rng"), P("dop")),
        out_specs=P("dop", None, "rng"),
        check_vma=False,
    )
```

time: 513 us -> 187 us (0.36); the launches traced: 503 us -> 187 us
  waiting for transfers between devices: 212 us -> 70.5 us
  other arithmetic: 131 us -> 2.47 us
  blocking collectives: 88 us -> 37.5 us
  Pallas kernels: 0 us -> 43.4 us
  between operations: 17.8 us -> 0.75 us
  matrix products: 26.5 us -> 9.59 us
  local copies, waits for them, and re-layouts: 19 us -> 6.03 us
  starting transfers between devices: 9.18 us -> 16.7 us
    another operation x20 -> x2, other arithmetic: 121 us -> 2.27 us  [the longest x14 78.8 us: solve_weights(): lower = jnp.linalg.cholesky(full_matrix)]
    reduce_scatter x1 -> x0, waiting for transfers between devices: 115 us -> none  [on_device(): lax.psum_scatter(covariance(snapshot, rows_mask), 'rng', scatter_dimensio...]
    unnamed x1 -> x0, blocking collectives: 62.2 us -> none
    pallas_call x0 -> x1, Pallas kernels: none -> 43.4 us  [full(): pl.pallas_call(functools.partial(full_kernel, gj, parts), out_shape=jax.S...]
    all_to_all x1, waiting for transfers between devices: 96.8 us -> 70.5 us  [on_device(): lax.all_to_all(spectrum, ('dop', 'rng'), split_axis=0, concat_axis=0, til...]
    all_to_all x0 -> x1, blocking collectives: none -> 12.9 us  [on_device(): return lax.all_to_all(beams, 'rng', split_axis=0, concat_axis=0, tiled=True)]
    dot_general x2 -> x0, matrix products: 12.1 us -> none  [the longest x1 9.01 us: covariance(): jnp.einsum('bkir,bjr->bkij', left_side, stacked, preferred_element_type=j...]
    another operation x19 -> x1, local copies, waits for them, and re-layouts: 8.02 us -> 0.13 us  [steering(): pair = jnp.stack([jnp.cos(phase_angle), jnp.sin(phase_angle)], 1)]
  transfers between devices with their start and end apart: 2 -> 1, of which waited for: 2 -> 1; matrix products, arithmetic and copies ran while one was open for 0% -> 0% of each run, Pallas kernels for 0% -> 0%
where the time goes in v1:
time: 187 us
  waiting for transfers between devices  70.5 us (38%)
  Pallas kernels  43.4 us (23%)
  blocking collectives  37.5 us (20%)
  starting transfers between devices  16.7 us (9%)
  matrix products  9.59 us (5%)
  local copies, waits for them, and re-layouts  6.03 us (3%)
  other arithmetic  2.47 us (1%)
    all_to_all x1, waiting for transfers between devices, on_device(): lax.all_to_all(spectrum, ('dop', 'rng'), split_axis=0, concat_axis=0, til...  70.5 us
    pallas_call x1, Pallas kernels, full(): pl.pallas_call(functools.partial(full_kernel, gj, parts), out_shape=jax.S...  43.4 us
    all_gather x1, blocking collectives, on_device(): mask = 1.0 - lax.all_gather(guard, 'rng', axis=0).astype(jnp.float32)  24.5 us
    all_to_all x1, starting transfers between devices, on_device(): lax.all_to_all(spectrum, ('dop', 'rng'), split_axis=0, concat_axis=0, til...  16.7 us
    all_to_all x1, blocking collectives, on_device(): return lax.all_to_all(beams, 'rng', split_axis=0, concat_axis=0, tiled=True)  12.9 us
    dot_general x1, matrix products, on_device(): jnp.einsum('kjpb,jpcr->bkcr', table, pulses, preferred_element_type=jnp.f...  9.59 us
    convert_element_type x1, local copies, waits for them, and re-layouts, on_device(): spectrum = jnp.einsum('kjpb,jpcr->bkcr', table, pulses, preferred_element...  4.67 us
  transfers between devices with their start and end apart: 1, of which 1 were waited for; matrix products, arithmetic and copies ran while one was open for 0% of the time, Pallas kernels for 0%

profile of v1, /device:TPU:1, one launch (start us, length us, event | category | flops | bytes accessed | tf_op | source)
XLA Modules:
  0.0 186.8 jit_solution(2206641354898774144)
XLA Ops:
  0.0 2.3 %fusion.14 = (bf16[1,512,256]{1,2,0:T(8,128)(2,1)S(1)}, bf16[1,512,256]{1,2,0:T(8,128)(2,1)S(1)}, bf16[1,512,256]{1,2,0:T(8,128)(2,1)S(1)}) fusion(f32[512]{0:T(512)S(1)} %multiply_subtract_fusion), kind=kLoop, calls=%fused_computation.22 | loop fusion | flops 2621440 | bytes 788480 | tf_op jit(solution)/shard_map/convert.7
  2.3 0.1 maximum_bitcast_fusion.2
  2.4 9.6 %fusion.3 = bf16[256,2,32,128]{3,0,2,1:T(8,128)(2,1)S(1)} fusion(bf16[2,512,32,128]{3,2,1,0:T(8,128)(2,1)} %param.3, bf16[1,2,512,256]{2,3,1,0:T(8,128)(2,1)S(1)} %get-tuple-element.6, bf16[1,2,512,256]{2,3,1,0:T(8,128)(2,1)S(1)} %get-tuple-element.5), kind=kOutput, calls=%fused_computation.4 | convolution fusion | flops 4299161600 | bytes 13631488 | tf_op jit(solution)/shard_map/kjpb,jpcr->bkcr/dot_general | solution.py:187
  12.0 4.7 %copy.8 = bf16[256,2,32,128]{3,2,1,0:T(8,128)(2,1)} copy(bf16[256,2,32,128]{3,0,2,1:T(8,128)(2,1)S(1)} %fusion.3) | data formatting | bytes 8388608 | tf_op jit(solution)/shard_map/convert_element_type | solution.py:189
  16.7 0.0 copy-start.1
  16.7 0.0 copy-start
  16.7 16.7 %all-to-all-start = ((bf16[256,2,32,128]{3,2,1,0:T(8,128)(2,1)}), bf16[256,2,32,128]{3,2,1,0:T(8,128)(2,1)}, u32[]{:S(2)}, u32[]{:S(2)}) async-start(bf16[256,2,32,128]{3,2,1,0:T(8,128)(2,1)} %copy.8), calls=%async_computation | async-start | bytes 8388608 | tf_op jit(solution)/shard_map/all_to_all | solution.py:192
  33.4 0.0 copy-done.1
  33.4 0.6 dynamic_slice.3
  34.6 0.1 fusion.15
  34.7 0.1 copy.10
  34.9 0.0 copy-done
  34.9 24.5 %all-gather.1 = s32[32,1,128]{2,1,0:T(1,128)S(1)} all-gather(s32[1,1,128]{2,1,0:T(1,128)S(1)} %bitcast.28), channel_id=2, replica_groups=mesh['rng'=32,'dop'=8] {'rng'}, dimensions={0}, use_global_device_ids=true | all-gather | bytes 16896 | tf_op jit(solution)/shard_map/all_gather | solution.py:190
  59.4 70.5 %all-to-all-done = bf16[256,2,32,128]{3,2,1,0:T(8,128)(2,1)} async-done(((bf16[256,2,32,128]{3,2,1,0:T(8,128)(2,1)}), bf16[256,2,32,128]{3,2,1,0:T(8,128)(2,1)}, u32[]{:S(2)}, u32[]{:S(2)}) %all-to-all-start) | async-done | bytes 4194336 | tf_op jit(solution)/shard_map/all_to_all | solution.py:192
  129.9 43.4 %solve.1 = f32[32,2,128]{2,1,0:T(2,128)S(1)} custom-call(bf16[8,32,64,128]{3,2,1,0:T(8,128)(2,1)} %bitcast.8.x_ref, f32[32,128]{1,0:T(8,128)S(1)} %subtract_bitcast_fusion.m_ref, f32[256,128]{1,0:T(8,128)S(1)} %pad.4.rhs_ref), custom_call_target="tpu_custom_call" | custom-call | tf_op jit(solution)/shard_map/solve/pallas_call | solution.py:146
  173.3 12.9 %all_to_all.10 = f32[32,2,128]{2,1,0:T(2,128)S(1)} all-to-all(f32[32,2,128]{2,1,0:T(2,128)S(1)} %solve.1), channel_id=1, replica_groups=mesh['rng'=32,'dop'=8] {'rng'}, dimensions={0} | all-to-all | bytes 65536 | tf_op jit(solution)/shard_map/all_to_all | solution.py:194
  186.2 0.6 copy.20
  (4 shorter events, 0.1 us)
Async XLA Ops:
  16.7 16.7 %copy-start.1 = (s32[32]{0:T(128)S(1)}, s32[32]{0:T(128)}, u32[]{:S(2)}) copy-start(s32[32]{0:T(128)} %param.5) | copy-start | bytes 388
  16.7 18.2 %copy-start = (s32[128]{0:T(128)S(1)}, s32[128]{0:T(128)}, u32[]{:S(2)}) copy-start(s32[128]{0:T(128)} %param.4) | copy-start | bytes 1540
  16.7 113.2 %all-to-all-start = ((bf16[256,2,32,128]{3,2,1,0:T(8,128)(2,1)}), bf16[256,2,32,128]{3,2,1,0:T(8,128)(2,1)}, u32[]{:S(2)}, u32[]{:S(2)}) async-start(bf16[256,2,32,128]{3,2,1,0:T(8,128)(2,1)} %copy.8), calls=%async_computation | async-start | bytes 8388608 | tf_op jit(solution)/shard_map/all_to_all | solution.py:192

commit v2 on v0

v2 whole, which is shorter than its diff:
```python
import functools
import math

import jax
import jax.numpy as jnp
from jax import lax
from jax.experimental import pallas as pl
from jax.experimental.pallas import tpu as pltpu

CELLS = 4096
CH = 256
NB = 32
LANES = 128


def dot(a, b):
    return jnp.dot(a, b, precision=lax.Precision.HIGHEST, preferred_element_type=jnp.float32)


def lane(x, j):
    return jnp.broadcast_to(x[:, j : j + 1], x.shape)


def sub(x, j):
    return jnp.broadcast_to(x[j : j + 1, :], x.shape)


def cmul(a, b):
    return a[0] * b[0] - a[1] * b[1], a[0] * b[1] + a[1] * b[0]


def cjmul(a, b):
    return a[0] * b[0] + a[1] * b[1], a[0] * b[1] - a[1] * b[0]


def add(a, b):
    return a[0] + b[0], a[1] + b[1]


def dif(a, b):
    return a[0] - b[0], a[1] - b[1]


def scale(s, a):
    return s * a[0], s * a[1]


def gauss_jordan(ar, ai, base):
    row = lax.broadcasted_iota(jnp.int32, (8, LANES), 0)
    for j in range(0, NB, 4):
        g, jj = divmod(j, 8)
        at = base + j
        p = [(sub(ar[g], jj + i), sub(ai[g], jj + i)) for i in range(4)]

        def entry(i, k):
            return lane(p[i][0], at + k), lane(p[i][1], at + k)

        d = [lane(p[k][0], at + k) for k in range(4)]
        a01, a02, a03 = entry(0, 1), entry(0, 2), entry(0, 3)
        a12, a13, a23 = entry(1, 2), entry(1, 3), entry(2, 3)
        t1 = 1.0 / (d[0] * d[1] - (a01[0] * a01[0] + a01[1] * a01[1]))
        w00 = scale(t1, dif(scale(d[1], a02), cmul(a01, a12)))
        w01 = scale(t1, dif(scale(d[1], a03), cmul(a01, a13)))
        w10 = scale(t1, dif(scale(d[0], a12), cjmul(a01, a02)))
        w11 = scale(t1, dif(scale(d[0], a13), cjmul(a01, a03)))
        s00 = d[2] - (cjmul(a02, w00)[0] + cjmul(a12, w10)[0])
        s11 = d[3] - (cjmul(a03, w01)[0] + cjmul(a13, w11)[0])
        s01 = dif(a23, add(cjmul(a02, w01), cjmul(a12, w11)))
        t2 = 1.0 / (s00 * s11 - (s01[0] * s01[0] + s01[1] * s01[1]))
        m0 = scale(t1, dif(scale(d[1], p[0]), cmul(a01, p[1])))
        m1 = scale(t1, dif(scale(d[0], p[1]), cjmul(a01, p[0])))
        q2 = dif(p[2], add(cjmul(a02, m0), cjmul(a12, m1)))
        q3 = dif(p[3], add(cjmul(a03, m0), cjmul(a13, m1)))
        n2 = scale(t2, dif(scale(s11, q2), cmul(s01, q3)))
        n3 = scale(t2, dif(scale(s00, q3), cjmul(s01, q2)))
        n0 = dif(m0, add(cmul(w00, n2), cmul(w01, n3)))
        n1 = dif(m1, add(cmul(w10, n2), cmul(w11, n3)))
        new = [n0, n1, n2, n3]
        br, bi = [], []
        for h in range(NB // 8):
            c = [(lane(ar[h], at + k), lane(ai[h], at + k)) for k in range(4)]
            u = add(add(cmul(c[0], n0), cmul(c[1], n1)), add(cmul(c[2], n2), cmul(c[3], n3)))
            ur, ui = ar[h] - u[0], ai[h] - u[1]
            if h == g:
                for i in range(4):
                    ur = jnp.where(row == jj + i, new[i][0], ur)
                    ui = jnp.where(row == jj + i, new[i][1], ui)
            br.append(ur)
            bi.append(ui)
        ar, ai = br, bi
    return ar, ai


def times_i(x, n):
    tail = x[:, 2 * n :]
    lane_no = lax.broadcasted_iota(jnp.int32, tail.shape, 1)
    back, fwd = pltpu.roll(tail, LANES - 1, 1), pltpu.roll(tail, 1, 1)
    return jnp.concatenate([-x[:, n : 2 * n], x[:, :n], jnp.where(lane_no == 0, -back, fwd)], 1)


def solve_in(w_ref):
    lanes = lax.broadcasted_iota(jnp.int32, (8, LANES), 1)
    rows = lax.broadcasted_iota(jnp.int32, (8, LANES), 0)
    dr, di = w_ref[:NB, :LANES], w_ref[:NB, CH : CH + LANES]
    for k in range(CH // NB):
        t, u = divmod(k, LANES // NB)
        base, other = NB * u, NB * ((u + 1) % (LANES // NB))
        inside = (lanes >= base) & (lanes < base + NB)
        ar, ai = [], []
        for h in range(NB // 8):
            unit = jnp.where(lanes == other + 8 * h + rows, 1.0, 0.0)
            ar.append(jnp.where(inside, dr[8 * h : 8 * h + 8], unit))
            ai.append(jnp.where(inside, di[8 * h : 8 * h + 8], 0.0))
        ar, ai = gauss_jordan(ar, ai, base)
        ar, ai = jnp.concatenate(ar, 0), jnp.concatenate(ai, 0)
        inv = jnp.concatenate([ar[:, other : other + NB], ai[:, other : other + NB]], 1)
        mine = slice(NB * k, NB * k + NB)
        live = slice(LANES * t, CH), slice(CH + LANES * t, 2 * CH), slice(2 * CH, 2 * CH + LANES)
        n = CH - LANES * t
        x = jnp.concatenate([w_ref[mine, s] for s in live], 1)
        y = dot(inv, jnp.concatenate([x, times_i(x, n)], 0))
        yy = jnp.concatenate([y, times_i(y, n)], 0)
        at = LANES * t + base
        c = jnp.concatenate([w_ref[:, at : at + NB], w_ref[:, CH + at : CH + at + NB]], 1)
        if k + 1 < CH // NB:
            nxt = slice(NB * k + NB, NB * k + 2 * NB)
            o = LANES * ((k + 1) // (LANES // NB) - t)
            e = LANES * t + o
            both = jnp.concatenate([yy[:, o : o + LANES], yy[:, n + o : n + o + LANES]], 1)
            step = dot(c[nxt], both)
            dr = w_ref[nxt, e : e + LANES] - step[:, :LANES]
            di = w_ref[nxt, CH + e : CH + e + LANES] - step[:, LANES:]
        upd = dot(c, yy)
        for s, o, m in zip(live, (0, n, 2 * n), (n, n, LANES)):
            w_ref[:, s] = w_ref[:, s] - upd[:, o : o + m]
            w_ref[mine, s] = y[:, o : o + m]


def cells_of(x_ref, s):
    x = x_ref[:, s]
    return x[:, :32].reshape(CH, LANES), x[:, 32:].reshape(CH, LANES)


UNROLL = 8


def cov_in(x_ref, m_ref, rhs_ref, w_ref, acc_ref):
    acc_ref[...] = jnp.zeros_like(acc_ref)

    def step(i, _):
        a, b = [], []
        for t in range(UNROLL):
            s = i * UNROLL + t
            xr, xi = cells_of(x_ref, s)
            m = jnp.broadcast_to(m_ref[pl.ds(s, 1), :].astype(jnp.bfloat16), (CH, LANES))
            xr, xi = xr * m, xi * m
            a += [xr, xi]
            b += [xi, -xr]
        a, b = jnp.concatenate(a, 1), jnp.concatenate(b, 1)
        acc_ref[...] += lax.dot_general(
            jnp.concatenate([a, b], 0), a, (((1,), (1,)), ((), ())), preferred_element_type=jnp.float32
        )
        return 0

    lax.fori_loop(0, CELLS // LANES // UNROLL, step, 0)
    re = acc_ref[:CH] * (1.0 / CELLS)
    im = acc_ref[CH:] * (1.0 / CELLS)
    diag = lax.broadcasted_iota(jnp.int32, (CH, CH), 0) == lax.broadcasted_iota(jnp.int32, (CH, CH), 1)
    loading = 0.1 * jnp.sum(jnp.where(diag, re, 0.0), keepdims=True) / CH + 1e-5
    w_ref[:, :CH] = re + jnp.where(diag, loading, 0.0)
    w_ref[:, CH : 2 * CH] = im
    w_ref[:, 2 * CH :] = rhs_ref[...]
    return loading


def beams_out(x_ref, m_ref, w_ref, loading, out_ref):
    wt = jnp.transpose(w_ref[:, 2 * CH :])[:8]
    wt = wt.astype(jnp.bfloat16).astype(jnp.float32)
    wr, wi = wt[0:1], wt[1:2]
    first = lax.broadcasted_iota(jnp.int32, (8, CH), 0)
    left = jnp.where(first == 0, wr, jnp.where(first == 1, -wi, 0.0))
    right = jnp.where(first == 0, wi, jnp.where(first == 1, wr, 0.0))
    lhs = jnp.concatenate([left, right], 1).astype(jnp.bfloat16)

    def step(i, p):
        x = []
        for t in range(UNROLL):
            x.append(jnp.concatenate(cells_of(x_ref, i * UNROLL + t), 0))
        raw = jnp.dot(lhs, jnp.concatenate(x, 1), preferred_element_type=jnp.float32)
        for t in range(UNROLL):
            s = i * UNROLL + t
            r = raw[:, LANES * t : LANES * t + LANES]
            out_ref[s] = r[:2]
            p = p + r * r * m_ref[pl.ds(s, 1), :]
        return p

    p = lax.fori_loop(0, CELLS // LANES // UNROLL, step, jnp.zeros((8, LANES), jnp.float32))
    sq = jnp.sum(jnp.where(first < 2, wt * wt, 0.0), keepdims=True)
    power = jnp.sum(p, keepdims=True) * (1.0 / CELLS) + loading * sq
    out_ref[...] = out_ref[...] * lax.rsqrt(power).reshape(1, 1, 1)


def bin_kernel(x_ref, m_ref, rhs_ref, out_ref, w_ref, acc_ref):
    loading = cov_in(x_ref, m_ref, rhs_ref, w_ref, acc_ref)
    solve_in(w_ref)
    beams_out(x_ref, m_ref, w_ref, loading, out_ref)


def one_bin(x, m, rhs):
    return pl.pallas_call(
        bin_kernel,
        out_shape=jax.ShapeDtypeStruct((CELLS // LANES, 2, LANES), jnp.float32),
        in_specs=[pl.BlockSpec(memory_space=pltpu.VMEM)] * 3,
        out_specs=pl.BlockSpec(memory_space=pltpu.VMEM),
        scratch_shapes=[
            pltpu.VMEM((CH, 2 * CH + LANES), jnp.float32),
            pltpu.VMEM((2 * CH, CH), jnp.float32),
        ],
        compiler_params=pltpu.CompilerParams(vmem_limit_bytes=40 * 2**20),
        name="one_bin",
    )(x, m, rhs)


from jax.sharding import PartitionSpec as P

NANG = 64


def doppler_table(period, bins):
    pulse_index = jnp.arange(period, dtype=jnp.int32)
    bin_index = jnp.arange(bins, dtype=jnp.int32)
    turn_count = pulse_index[:, None] * bin_index[None, :] % period
    phase_angle = 2.0 * math.pi / period * turn_count.astype(jnp.float32)
    window_taper = 0.54 - 0.46 * jnp.cos(
        2.0 * math.pi / (period - 1) * pulse_index.astype(jnp.float32)
    )
    cosine = window_taper[:, None] * jnp.cos(phase_angle)
    sine_part = window_taper[:, None] * jnp.sin(phase_angle)
    return jnp.stack([jnp.stack([cosine, sine_part]), jnp.stack([-sine_part, cosine])]).astype(
        jnp.bfloat16
    )


def steering(index, channels):
    sine_of = -0.9 + 1.8 * index.astype(jnp.float32) / (NANG - 1)
    phase_angle = math.pi * jnp.arange(channels, dtype=jnp.float32) * sine_of
    pair = jnp.stack([jnp.cos(phase_angle), jnp.sin(phase_angle)], 1)
    return jnp.pad(pair, ((0, 0), (0, LANES - 2)))


def on_device(pulses, guard, steer_index):
    bins = steer_index.shape[0] * lax.axis_size("dop")
    table = doppler_table(pulses.shape[1], bins)
    spectrum = jnp.einsum(
        "kjpb,jpcr->bkcr", table, pulses, preferred_element_type=jnp.float32
    ).astype(jnp.bfloat16)
    mask = 1.0 - lax.all_gather(guard, "rng", axis=0).astype(jnp.float32)
    rhs = steering(steer_index[lax.axis_index("rng")], CH)
    whole = lax.all_to_all(spectrum, ("dop", "rng"), split_axis=0, concat_axis=0, tiled=True)
    beams = one_bin(whole.reshape(8, CELLS // LANES, 64, LANES), mask, rhs)
    return lax.all_to_all(beams, "rng", split_axis=0, concat_axis=0, tiled=True)


def solution(mesh):
    return jax.shard_map(
        on_device,
        mesh=mesh,
        in_specs=(P(None, None, "dop", "rng"), P("rng"), P("dop")),
        out_specs=P("dop", None, "rng"),
        check_vma=False,
    )
```

time: 513 us -> 167 us (0.33); the launches traced: 503 us -> 167 us
  waiting for transfers between devices: 212 us -> 70.5 us
  other arithmetic: 131 us -> 2.47 us
  blocking collectives: 88 us -> 37.3 us
  Pallas kernels: 0 us -> 23.4 us
  between operations: 17.8 us -> 0.75 us
  matrix products: 26.5 us -> 9.6 us
  local copies, waits for them, and re-layouts: 19 us -> 6.03 us
  starting transfers between devices: 9.18 us -> 16.6 us
    another operation x20 -> x2, other arithmetic: 121 us -> 2.27 us  [the longest x14 78.8 us: solve_weights(): lower = jnp.linalg.cholesky(full_matrix)]
    reduce_scatter x1 -> x0, waiting for transfers between devices: 115 us -> none  [on_device(): lax.psum_scatter(covariance(snapshot, rows_mask), 'rng', scatter_dimensio...]
    unnamed x1 -> x0, blocking collectives: 62.2 us -> none
    all_to_all x1, waiting for transfers between devices: 96.8 us -> 70.5 us  [on_device(): lax.all_to_all(spectrum, ('dop', 'rng'), split_axis=0, concat_axis=0, til...]
    pallas_call x0 -> x1, Pallas kernels: none -> 23.4 us  [one_bin(): pl.pallas_call(bin_kernel, out_shape=jax.ShapeDtypeStruct((CELLS // LANES...]
    all_to_all x0 -> x1, blocking collectives: none -> 12.8 us  [on_device(): return lax.all_to_all(beams, 'rng', split_axis=0, concat_axis=0, tiled=True)]
    dot_general x2 -> x0, matrix products: 12.1 us -> none  [the longest x1 9.01 us: covariance(): jnp.einsum('bkir,bjr->bkij', left_side, stacked, preferred_element_type=j...]
    another operation x19 -> x1, local copies, waits for them, and re-layouts: 8.02 us -> 0.13 us  [steering(): pair = jnp.stack([jnp.cos(phase_angle), jnp.sin(phase_angle)], 1)]
  transfers between devices with their start and end apart: 2 -> 1, of which waited for: 2 -> 1; matrix products, arithmetic and copies ran while one was open for 0% -> 0% of each run, Pallas kernels for 0% -> 0%
where the time goes in v2:
time: 167 us
  waiting for transfers between devices  70.5 us (42%)
  blocking collectives  37.3 us (22%)
  Pallas kernels  23.4 us (14%)
  starting transfers between devices  16.6 us (10%)
  matrix products  9.6 us (6%)
  local copies, waits for them, and re-layouts  6.03 us (4%)
  other arithmetic  2.47 us (1%)
    all_to_all x1, waiting for transfers between devices, on_device(): lax.all_to_all(spectrum, ('dop', 'rng'), split_axis=0, concat_axis=0, til...  70.5 us
    all_gather x1, blocking collectives, on_device(): mask = 1.0 - lax.all_gather(guard, 'rng', axis=0).astype(jnp.float32)  24.5 us
    pallas_call x1, Pallas kernels, one_bin(): pl.pallas_call(bin_kernel, out_shape=jax.ShapeDtypeStruct((CELLS // LANES...  23.4 us
    all_to_all x1, starting transfers between devices, on_device(): lax.all_to_all(spectrum, ('dop', 'rng'), split_axis=0, concat_axis=0, til...  16.6 us
    all_to_all x1, blocking collectives, on_device(): return lax.all_to_all(beams, 'rng', split_axis=0, concat_axis=0, tiled=True)  12.8 us
    dot_general x1, matrix products, on_device(): jnp.einsum('kjpb,jpcr->bkcr', table, pulses, preferred_element_type=jnp.f...  9.6 us
    convert_element_type x1, local copies, waits for them, and re-layouts, on_device(): spectrum = jnp.einsum('kjpb,jpcr->bkcr', table, pulses, preferred_element...  4.67 us
  transfers between devices with their start and end apart: 1, of which 1 were waited for; matrix products, arithmetic and copies ran while one was open for 0% of the time, Pallas kernels for 0%

profile of v2, /device:TPU:1, one launch (start us, length us, event | category | flops | bytes accessed | tf_op | source)
XLA Modules:
  0.0 166.7 jit_solution(11195663219059940546)
XLA Ops:
  0.0 2.3 %fusion.14 = (bf16[1,512,256]{1,2,0:T(8,128)(2,1)S(1)}, bf16[1,512,256]{1,2,0:T(8,128)(2,1)S(1)}, bf16[1,512,256]{1,2,0:T(8,128)(2,1)S(1)}) fusion(f32[512]{0:T(512)S(1)} %multiply_subtract_fusion), kind=kLoop, calls=%fused_computation.22 | loop fusion | flops 2621440 | bytes 788480 | tf_op jit(solution)/shard_map/convert.7
  2.3 0.1 maximum_bitcast_fusion.2
  2.4 9.6 %fusion.3 = bf16[256,2,32,128]{3,0,2,1:T(8,128)(2,1)S(1)} fusion(bf16[2,512,32,128]{3,2,1,0:T(8,128)(2,1)} %param.3, bf16[1,2,512,256]{2,3,1,0:T(8,128)(2,1)S(1)} %get-tuple-element.6, bf16[1,2,512,256]{2,3,1,0:T(8,128)(2,1)S(1)} %get-tuple-element.5), kind=kOutput, calls=%fused_computation.4 | convolution fusion | flops 4299161600 | bytes 13631488 | tf_op jit(solution)/shard_map/kjpb,jpcr->bkcr/dot_general | solution.py:254
  12.0 4.7 %copy.8 = bf16[256,2,32,128]{3,2,1,0:T(8,128)(2,1)} copy(bf16[256,2,32,128]{3,0,2,1:T(8,128)(2,1)S(1)} %fusion.3) | data formatting | bytes 8388608 | tf_op jit(solution)/shard_map/convert_element_type | solution.py:256
  16.7 0.0 copy-start.1
  16.7 0.0 copy-start
  16.7 16.6 %all-to-all-start = ((bf16[256,2,32,128]{3,2,1,0:T(8,128)(2,1)}), bf16[256,2,32,128]{3,2,1,0:T(8,128)(2,1)}, u32[]{:S(2)}, u32[]{:S(2)}) async-start(bf16[256,2,32,128]{3,2,1,0:T(8,128)(2,1)} %copy.8), calls=%async_computation | async-start | bytes 8388608 | tf_op jit(solution)/shard_map/all_to_all | solution.py:259
  33.4 0.0 copy-done.1
  33.4 0.6 dynamic_slice.3
  34.6 0.1 fusion.15
  34.7 0.1 copy.10
  34.8 0.0 copy-done
  34.9 24.5 %all-gather.1 = s32[32,1,128]{2,1,0:T(1,128)S(1)} all-gather(s32[1,1,128]{2,1,0:T(1,128)S(1)} %bitcast.28), channel_id=2, replica_groups=mesh['rng'=32,'dop'=8] {'rng'}, dimensions={0}, use_global_device_ids=true | all-gather | bytes 16896 | tf_op jit(solution)/shard_map/all_gather | solution.py:257
  59.4 70.5 %all-to-all-done = bf16[256,2,32,128]{3,2,1,0:T(8,128)(2,1)} async-done(((bf16[256,2,32,128]{3,2,1,0:T(8,128)(2,1)}), bf16[256,2,32,128]{3,2,1,0:T(8,128)(2,1)}, u32[]{:S(2)}, u32[]{:S(2)}) %all-to-all-start) | async-done | bytes 4194336 | tf_op jit(solution)/shard_map/all_to_all | solution.py:259
  129.9 23.4 %one_bin.1 = f32[32,2,128]{2,1,0:T(2,128)S(1)} custom-call(bf16[8,32,64,128]{3,2,1,0:T(8,128)(2,1)} %bitcast.8.x_ref, f32[32,128]{1,0:T(8,128)S(1)} %subtract_bitcast_fusion.m_ref, f32[256,128]{1,0:T(8,128)S(1)} %pad.4.rhs_ref), custom_call_target="tpu_custom_call" | custom-call | tf_op jit(solution)/shard_map/one_bin/pallas_call | solution.py:210
  153.3 12.8 %all_to_all.10 = f32[32,2,128]{2,1,0:T(2,128)S(1)} all-to-all(f32[32,2,128]{2,1,0:T(2,128)S(1)} %one_bin.1), channel_id=1, replica_groups=mesh['rng'=32,'dop'=8] {'rng'}, dimensions={0} | all-to-all | bytes 65536 | tf_op jit(solution)/shard_map/all_to_all | solution.py:261
  166.1 0.6 copy.20
  (4 shorter events, 0.1 us)
Async XLA Ops:
  16.7 16.7 %copy-start.1 = (s32[32]{0:T(128)S(1)}, s32[32]{0:T(128)}, u32[]{:S(2)}) copy-start(s32[32]{0:T(128)} %param.5) | copy-start | bytes 388
  16.7 18.2 %copy-start = (s32[128]{0:T(128)S(1)}, s32[128]{0:T(128)}, u32[]{:S(2)}) copy-start(s32[128]{0:T(128)} %param.4) | copy-start | bytes 1540
  16.7 113.2 %all-to-all-start = ((bf16[256,2,32,128]{3,2,1,0:T(8,128)(2,1)}), bf16[256,2,32,128]{3,2,1,0:T(8,128)(2,1)}, u32[]{:S(2)}, u32[]{:S(2)}) async-start(bf16[256,2,32,128]{3,2,1,0:T(8,128)(2,1)} %copy.8), calls=%async_computation | async-start | bytes 8388608 | tf_op jit(solution)/shard_map/all_to_all | solution.py:259

commit v3 on v2

--- a/solution.py
+++ b/solution.py
@@ -3,6 +3,8 @@
 
 import jax
 import jax.numpy as jnp
+import ml_dtypes
+import numpy as np
 from jax import lax
 from jax.experimental import pallas as pl
 from jax.experimental.pallas import tpu as pltpu
@@ -11,6 +13,9 @@
 CH = 256
 NB = 32
 LANES = 128
+HBM = pltpu.MemorySpace.HBM
+VMEM_LIMIT = 60 * 2**20
+SLOTS = 10
 
 
 def dot(a, b):
@@ -45,17 +50,28 @@
     return s * a[0], s * a[1]
 
 
-def gauss_jordan(ar, ai, base):
+def gauss_jordan(ar, ai, base, s_ref):
     row = lax.broadcasted_iota(jnp.int32, (8, LANES), 0)
     for j in range(0, NB, 4):
         g, jj = divmod(j, 8)
         at = base + j
-        p = [(sub(ar[g], jj + i), sub(ai[g], jj + i)) for i in range(4)]
+        slot = SLOTS * ((j // 4) % 2)
+
+        def spread(k, i):
+            return jnp.broadcast_to(s_ref[slot + k, i : i + 1, :], (8, LANES))
+
+        col = [(lane(ar[g], at + k), lane(ai[g], at + k)) for k in range(4)]
+        s_ref[slot] = ar[g]
+        s_ref[slot + 1] = ai[g]
+        for k in range(4):
+            s_ref[slot + 2 + 2 * k] = col[k][0]
+            s_ref[slot + 3 + 2 * k] = col[k][1]
+        p = [(spread(0, jj + i), spread(1, jj + i)) for i in range(4)]
 
         def entry(i, k):
-            return lane(p[i][0], at + k), lane(p[i][1], at + k)
-
-        d = [lane(p[k][0], at + k) for k in range(4)]
+            return spread(2 + 2 * k, jj + i), spread(3 + 2 * k, jj + i)
+
+        d = [spread(2 + 2 * k, jj + k) for k in range(4)]
         a01, a02, a03 = entry(0, 1), entry(0, 2), entry(0, 3)
         a12, a13, a23 = entry(1, 2), entry(1, 3), entry(2, 3)
         t1 = 1.0 / (d[0] * d[1] - (a01[0] * a01[0] + a01[1] * a01[1]))
@@ -78,7 +94,7 @@
         new = [n0, n1, n2, n3]
         br, bi = [], []
         for h in range(NB // 8):
-            c = [(lane(ar[h], at + k), lane(ai[h], at + k)) for k in range(4)]
+            c = col if h == g else [(lane(ar[h], at + k), lane(ai[h], at + k)) for k in range(4)]
             u = add(add(cmul(c[0], n0), cmul(c[1], n1)), add(cmul(c[2], n2), cmul(c[3], n3)))
             ur, ui = ar[h] - u[0], ai[h] - u[1]
             if h == g:
@@ -98,7 +114,7 @@
     return jnp.concatenate([-x[:, n : 2 * n], x[:, :n], jnp.where(lane_no == 0, -back, fwd)], 1)
 
 
-def solve_in(w_ref):
+def solve_in(w_ref, s_ref):
     lanes = lax.broadcasted_iota(jnp.int32, (8, LANES), 1)
     rows = lax.broadcasted_iota(jnp.int32, (8, LANES), 0)
     dr, di = w_ref[:NB, :LANES], w_ref[:NB, CH : CH + LANES]
@@ -111,7 +127,7 @@
             unit = jnp.where(lanes == other + 8 * h + rows, 1.0, 0.0)
             ar.append(jnp.where(inside, dr[8 * h : 8 * h + 8], unit))
             ai.append(jnp.where(inside, di[8 * h : 8 * h + 8], 0.0))
-        ar, ai = gauss_jordan(ar, ai, base)
+        ar, ai = gauss_jordan(ar, ai, base, s_ref)
         ar, ai = jnp.concatenate(ar, 0), jnp.concatenate(ai, 0)
         inv = jnp.concatenate([ar[:, other : other + NB], ai[:, other : other + NB]], 1)
         mine = slice(NB * k, NB * k + NB)
@@ -137,17 +153,18 @@
 
 
 def cells_of(x_ref, s):
-    x = x_ref[:, s]
+    x = x_ref[s]
     return x[:, :32].reshape(CH, LANES), x[:, 32:].reshape(CH, LANES)
 
 
 UNROLL = 8
 
 
-def cov_in(x_ref, m_ref, rhs_ref, w_ref, acc_ref):
+def cov_in(x_ref, m_ref, rhs_ref, w_ref, acc_ref, arrive):
     acc_ref[...] = jnp.zeros_like(acc_ref)
 
     def step(i, _):
+        arrive(i)
         a, b = [], []
         for t in range(UNROLL):
             s = i * UNROLL + t
@@ -200,9 +217,15 @@
     out_ref[...] = out_ref[...] * lax.rsqrt(power).reshape(1, 1, 1)
 
 
-def bin_kernel(x_ref, m_ref, rhs_ref, out_ref, w_ref, acc_ref):
-    loading = cov_in(x_ref, m_ref, rhs_ref, w_ref, acc_ref)
-    solve_in(w_ref)
+def bin_kernel(x_hbm, m_ref, rhs_ref, out_ref, x_ref, w_ref, acc_ref, s_ref, in_sem):
+    def fetch(i):
+        rows = pl.ds(i * UNROLL, UNROLL)
+        return pltpu.make_async_copy(x_hbm.at[rows], x_ref.at[rows], in_sem.at[i])
+
+    for i in range(CELLS // LANES // UNROLL):
+        fetch(i).start()
+    loading = cov_in(x_ref, m_ref, rhs_ref, w_ref, acc_ref, lambda i: fetch(i).wait())
+    solve_in(w_ref, s_ref)
     beams_out(x_ref, m_ref, w_ref, loading, out_ref)
 
 
@@ -210,35 +233,121 @@
     return pl.pallas_call(
         bin_kernel,
         out_shape=jax.ShapeDtypeStruct((CELLS // LANES, 2, LANES), jnp.float32),
-        in_specs=[pl.BlockSpec(memory_space=pltpu.VMEM)] * 3,
+        in_specs=[pl.BlockSpec(memory_space=HBM)] + [pl.BlockSpec(memory_space=pltpu.VMEM)] * 2,
         out_specs=pl.BlockSpec(memory_space=pltpu.VMEM),
         scratch_shapes=[
+            pltpu.VMEM(x.shape, x.dtype),
             pltpu.VMEM((CH, 2 * CH + LANES), jnp.float32),
             pltpu.VMEM((2 * CH, CH), jnp.float32),
+            pltpu.VMEM((2 * SLOTS, 8, LANES), jnp.float32),
+            pltpu.SemaphoreType.DMA((CELLS // LANES // UNROLL,)),
         ],
-        compiler_params=pltpu.CompilerParams(vmem_limit_bytes=40 * 2**20),
+        compiler_params=pltpu.CompilerParams(vmem_limit_bytes=VMEM_LIMIT),
         name="one_bin",
     )(x, m, rhs)
 
 
+GROUP = 16
+IN_STRIDE = 24
+OUT_STRIDE = 40
+
+
+def doppler_rows(period, bins, blocks):
+    pulse_index = np.arange(period, dtype=np.int32)
+    bin_index = np.arange(bins, dtype=np.int32).reshape(blocks, -1).T.reshape(-1)
+    turn_count = bin_index[:, None] * pulse_index[None, :] % period
+    phase_angle = np.float32(2.0 * math.pi / period) * turn_count.astype(np.float32)
+    window_taper = np.float32(0.54) - np.float32(0.46) * np.cos(
+        np.float32(2.0 * math.pi / (period - 1)) * pulse_index.astype(np.float32)
+    )
+    cosine = window_taper * np.cos(phase_angle)
+    sine_part = window_taper * np.sin(phase_angle)
+    return np.concatenate(
+        [np.concatenate([cosine, sine_part], 1), np.concatenate([-sine_part, cosine], 1)], 0
+    ).astype(ml_dtypes.bfloat16)
+
+
+PIECES = 4
+
+
+def transform_kernel(
+    table_hbm, x_hbm, out_hbm, table_ref, raw_ref, wide_ref, back_ref, out_ref, table_sem, in_sem, out_sem
+):
+    parts, pulses, channels = x_hbm.shape[:3]
+    depth, bins, groups = parts * pulses, out_hbm.shape[0], channels // GROUP
+    step = depth // PIECES
+
+    def fetch(g, i):
+        k, first = divmod(i * step, pulses)
+        return pltpu.make_async_copy(
+            x_hbm.at[k, pl.ds(first, step), pl.ds(GROUP * g, GROUP), :],
+            raw_ref.at[g, pl.ds(step * i, step)],
+            in_sem.at[g, i],
+        )
+
+    def send(g, k):
+        return pltpu.make_async_copy(
+            out_ref.at[g, k], out_hbm.at[:, k, pl.ds(GROUP * g, GROUP), :], out_sem.at[g, k]
+        )
+
+    table_copy = pltpu.make_async_copy(table_hbm, table_ref, table_sem)
+    for g in range(groups):
+        for i in range(PIECES):
+            fetch(g, i).start()
+        if g == 0:
+            table_copy.start()
+    flat = wide_ref.reshape(depth * IN_STRIDE, LANES)
+    bflat = back_ref.reshape(bins * OUT_STRIDE, LANES)
+    for g in range(groups):
+        for i in range(PIECES):
+            fetch(g, i).wait()
+            rows = pl.ds(step * i, step)
+            wide_ref[rows, :GROUP] = raw_ref[g, rows].astype(jnp.float32)
+        if g == 0:
+            table_copy.wait()
+        for c in range(0, GROUP, 2):
+            x = [flat[pl.ds(c + i, depth, stride=IN_STRIDE), :].astype(jnp.bfloat16) for i in range(2)]
+            y = jnp.dot(table_ref[...], jnp.concatenate(x, 1), preferred_element_type=jnp.float32)
+            for k in range(2):
+                for i in range(2):
+                    bflat[pl.ds(k * GROUP + c + i, bins, stride=OUT_STRIDE), :] = y[
+                        bins * k : bins * k + bins, LANES * i : LANES * i + LANES
+                    ]
+        for k in range(2):
+            out_ref[g, k] = back_ref[:, k * GROUP : k * GROUP + GROUP].astype(jnp.bfloat16)
+            send(g, k).start()
+    for g in range(groups):
+        for k in range(2):
+            send(g, k).wait()
+
+
+def transform(pulses, bins, blocks):
+    parts, period, channels, cells = pulses.shape
+    table = jnp.asarray(doppler_rows(period, bins, blocks))
+    groups, depth = channels // GROUP, parts * period
+    return pl.pallas_call(
+        transform_kernel,
+        out_shape=jax.ShapeDtypeStruct((bins, 2, channels, cells), jnp.bfloat16),
+        in_specs=[pl.BlockSpec(memory_space=HBM)] * 2,
+        out_specs=pl.BlockSpec(memory_space=HBM),
+        scratch_shapes=[
+            pltpu.VMEM((2 * bins, depth), jnp.bfloat16),
+            pltpu.VMEM((groups, depth, GROUP, cells), jnp.bfloat16),
+            pltpu.VMEM((depth, IN_STRIDE, cells), jnp.float32),
+            pltpu.VMEM((bins, OUT_STRIDE, cells), jnp.float32),
+            pltpu.VMEM((groups, 2, bins, GROUP, cells), jnp.bfloat16),
+            pltpu.SemaphoreType.DMA,
+            pltpu.SemaphoreType.DMA((groups, PIECES)),
+            pltpu.SemaphoreType.DMA((groups, 2)),
+        ],
+        compiler_params=pltpu.CompilerParams(vmem_limit_bytes=VMEM_LIMIT),
+        name="transform",
+    )(table, pulses)
+
+
 from jax.sharding import PartitionSpec as P
 
 NANG = 64
-
-
-def doppler_table(period, bins):
-    pulse_index = jnp.arange(period, dtype=jnp.int32)
-    bin_index = jnp.arange(bins, dtype=jnp.int32)
-    turn_count = pulse_index[:, None] * bin_index[None, :] % period
-    phase_angle = 2.0 * math.pi / period * turn_count.astype(jnp.float32)
-    window_taper = 0.54 - 0.46 * jnp.cos(
-        2.0 * math.pi / (period - 1) * pulse_index.astype(jnp.float32)
-    )
-    cosine = window_taper[:, None] * jnp.cos(phase_angle)
-    sine_part = window_taper[:, None] * jnp.sin(phase_angle)
-    return jnp.stack([jnp.stack([cosine, sine_part]), jnp.stack([-sine_part, cosine])]).astype(
-        jnp.bfloat16
-    )
 
 
 def steering(index, channels):
@@ -250,14 +359,11 @@
 
 def on_device(pulses, guard, steer_index):
     bins = steer_index.shape[0] * lax.axis_size("dop")
-    table = doppler_table(pulses.shape[1], bins)
-    spectrum = jnp.einsum(
-        "kjpb,jpcr->bkcr", table, pulses, preferred_element_type=jnp.float32
-    ).astype(jnp.bfloat16)
+    spectrum = transform(pulses, bins, lax.axis_size("dop"))
     mask = 1.0 - lax.all_gather(guard, "rng", axis=0).astype(jnp.float32)
     rhs = steering(steer_index[lax.axis_index("rng")], CH)
-    whole = lax.all_to_all(spectrum, ("dop", "rng"), split_axis=0, concat_axis=0, tiled=True)
-    beams = one_bin(whole.reshape(8, CELLS // LANES, 64, LANES), mask, rhs)
+    whole = lax.all_to_all(spectrum, ("rng", "dop"), split_axis=0, concat_axis=0, tiled=True)
+    beams = one_bin(whole.reshape(CELLS // LANES, 8, 64, LANES), mask, rhs)
     return lax.all_to_all(beams, "rng", split_axis=0, concat_axis=0, tiled=True)
 
 

time: 167 us -> 159 us (0.952)
  matrix products: 9.6 us -> 0 us
  Pallas kernels: 23.4 us -> 31.7 us
  local copies, waits for them, and re-layouts: 6.03 us -> 2.01 us
  blocking collectives: 37.3 us -> 35 us
  other arithmetic: 2.47 us -> 0.67 us
    pallas_call x0 -> x1, Pallas kernels: none -> 11.1 us  [transform(): pl.pallas_call(transform_kernel, out_shape=jax.ShapeDtypeStruct((bins, 2,...]
    dot_general x1 -> x0, matrix products: 9.6 us -> none  [on_device(): jnp.einsum('kjpb,jpcr->bkcr', table, pulses, preferred_element_type=jnp.f...]
    convert_element_type x1 -> x0, local copies, waits for them, and re-layouts: 4.67 us -> none  [on_device(): spectrum = jnp.einsum('kjpb,jpcr->bkcr', table, pulses, preferred_element...]
    pallas_call x1, Pallas kernels: 23.4 us -> 20.7 us  [one_bin(): pl.pallas_call(bin_kernel, out_shape=jax.ShapeDtypeStruct((CELLS // LANES...]
    another operation x2 -> x0, other arithmetic: 2.35 us -> none
    all_gather x1, blocking collectives: 24.5 us -> 22.8 us  [on_device(): mask = 1.0 - lax.all_gather(guard, 'rng', axis=0).astype(jnp.float32)]
  transfers between devices with their start and end apart: 1 -> 1, of which waited for: 1 -> 1; matrix products, arithmetic and copies ran while one was open for 0% -> 1% of each run, Pallas kernels for 0% -> 0%
where the time goes in v3:
time: 159 us
  waiting for transfers between devices  71.9 us (45%)
  blocking collectives  35 us (22%)
  Pallas kernels  31.7 us (20%)
  starting transfers between devices  16.7 us (11%)
  local copies, waits for them, and re-layouts  2.01 us (1%)
    all_to_all x1, waiting for transfers between devices, on_device(): lax.all_to_all(spectrum, ('rng', 'dop'), split_axis=0, concat_axis=0, til...  71.9 us
    all_gather x1, blocking collectives, on_device(): mask = 1.0 - lax.all_gather(guard, 'rng', axis=0).astype(jnp.float32)  22.8 us
    pallas_call x1, Pallas kernels, one_bin(): pl.pallas_call(bin_kernel, out_shape=jax.ShapeDtypeStruct((CELLS // LANES...  20.7 us
    all_to_all x1, starting transfers between devices, on_device(): lax.all_to_all(spectrum, ('rng', 'dop'), split_axis=0, concat_axis=0, til...  16.7 us
    all_to_all x1, blocking collectives, on_device(): return lax.all_to_all(beams, 'rng', split_axis=0, concat_axis=0, tiled=True)  12.2 us
    pallas_call x1, Pallas kernels, transform(): pl.pallas_call(transform_kernel, out_shape=jax.ShapeDtypeStruct((bins, 2,...  11.1 us
  transfers between devices with their start and end apart: 1, of which 1 were waited for; matrix products, arithmetic and copies ran while one was open for 1% of the time, Pallas kernels for 0%

profile of v3, /device:TPU:1, one launch (start us, length us, event | category | flops | bytes accessed | tf_op | source)
XLA Modules:
  0.0 158.7 jit_solution(9316717458208112573)
XLA Ops:
  0.0 11.1 %transform.1 = bf16[256,2,32,128]{3,2,1,0:T(8,128)(2,1)} custom-call(bf16[512,1024]{1,0:T(8,128)(2,1)} %constant.28.clone.table_hbm, bf16[2,512,32,128]{3,2,1,0:T(8,128)(2,1)} %x_hbm.1), custom_call_target="tpu_custom_call" | custom-call | tf_op jit(solution)/shard_map/transform/pallas_call | solution.py:328
  11.1 0.0 copy-start.1
  11.1 0.0 copy-start
  11.1 16.7 %all-to-all-start = ((bf16[256,2,32,128]{3,2,1,0:T(8,128)(2,1)}), bf16[256,2,32,128]{3,2,1,0:T(8,128)(2,1)}, u32[]{:S(2)}, u32[]{:S(2)}) async-start(bf16[256,2,32,128]{3,2,1,0:T(8,128)(2,1)} %transform.1), calls=%async_computation | async-start | bytes 8388608 | tf_op jit(solution)/shard_map/all_to_all | solution.py:365
  27.8 0.0 copy-done.1
  27.8 0.6 dynamic_slice.3
  29.0 0.1 fusion
  29.1 0.1 copy.7
  29.2 0.7 pad.4.rhs_ref
  29.9 0.0 copy-done
  29.9 22.8 %all-gather.1 = s32[32,1,128]{2,1,0:T(1,128)S(1)} all-gather(s32[1,1,128]{2,1,0:T(1,128)S(1)} %bitcast.7), channel_id=2, replica_groups=mesh['rng'=32,'dop'=8] {'rng'}, dimensions={0}, use_global_device_ids=true | all-gather | bytes 16896 | tf_op jit(solution)/shard_map/all_gather | solution.py:363
  52.7 0.6 subtract_bitcast_fusion.m_ref
  53.3 71.9 %all-to-all-done = bf16[256,2,32,128]{3,2,1,0:T(8,128)(2,1)} async-done(((bf16[256,2,32,128]{3,2,1,0:T(8,128)(2,1)}), bf16[256,2,32,128]{3,2,1,0:T(8,128)(2,1)}, u32[]{:S(2)}, u32[]{:S(2)}) %all-to-all-start) | async-done | bytes 4194336 | tf_op jit(solution)/shard_map/all_to_all | solution.py:365
  125.2 20.7 %one_bin.1 = f32[32,2,128]{2,1,0:T(2,128)} custom-call(bf16[32,8,64,128]{3,2,1,0:T(8,128)(2,1)} %bitcast.x_hbm, f32[32,128]{1,0:T(8,128)} %subtract_bitcast_fusion.m_ref, f32[256,128]{1,0:T(8,128)} %pad.4.rhs_ref), custom_call_target="tpu_custom_call" | custom-call | tf_op jit(solution)/shard_map/one_bin/pallas_call | solution.py:233
  145.9 12.2 %all_to_all.10 = f32[32,2,128]{2,1,0:T(2,128)S(1)} all-to-all(f32[32,2,128]{2,1,0:T(2,128)} %one_bin.1), channel_id=1, replica_groups=mesh['rng'=32,'dop'=8] {'rng'}, dimensions={0} | all-to-all | bytes 65536 | tf_op jit(solution)/shard_map/all_to_all | solution.py:367
  158.1 0.6 copy.9
  (1 shorter events, 0.0 us)
Async XLA Ops:
  11.1 16.7 %copy-start.1 = (s32[32]{0:T(128)S(1)}, s32[32]{0:T(128)}, u32[]{:S(2)}) copy-start(s32[32]{0:T(128)} %param.6) | copy-start | bytes 388
  11.1 18.8 %copy-start = (s32[128]{0:T(128)S(1)}, s32[128]{0:T(128)}, u32[]{:S(2)}) copy-start(s32[128]{0:T(128)} %param.5) | copy-start | bytes 1540
  11.1 114.2 %all-to-all-start = ((bf16[256,2,32,128]{3,2,1,0:T(8,128)(2,1)}), bf16[256,2,32,128]{3,2,1,0:T(8,128)(2,1)}, u32[]{:S(2)}, u32[]{:S(2)}) async-start(bf16[256,2,32,128]{3,2,1,0:T(8,128)(2,1)} %transform.1), calls=%async_computation | async-start | bytes 8388608 | tf_op jit(solution)/shard_map/all_to_all | solution.py:365

commit v4 on v3

--- a/solution.py
+++ b/solution.py
@@ -15,7 +15,8 @@
 LANES = 128
 HBM = pltpu.MemorySpace.HBM
 VMEM_LIMIT = 60 * 2**20
-SLOTS = 10
+SLOTS = 14
+PART = CH + LANES
 
 
 def dot(a, b):
@@ -50,7 +51,7 @@
     return s * a[0], s * a[1]
 
 
-def gauss_jordan(ar, ai, base, s_ref):
+def gauss_jordan(tiles, base, s_ref):
     row = lax.broadcasted_iota(jnp.int32, (8, LANES), 0)
     for j in range(0, NB, 4):
         g, jj = divmod(j, 8)
@@ -60,18 +61,21 @@
         def spread(k, i):
             return jnp.broadcast_to(s_ref[slot + k, i : i + 1, :], (8, LANES))
 
-        col = [(lane(ar[g], at + k), lane(ai[g], at + k)) for k in range(4)]
-        s_ref[slot] = ar[g]
-        s_ref[slot + 1] = ai[g]
+        def column(h):
+            return [(lane(tiles[0][h][0], at + k), lane(tiles[0][h][1], at + k)) for k in range(4)]
+
+        col = column(g)
         for k in range(4):
-            s_ref[slot + 2 + 2 * k] = col[k][0]
-            s_ref[slot + 3 + 2 * k] = col[k][1]
-        p = [(spread(0, jj + i), spread(1, jj + i)) for i in range(4)]
+            s_ref[slot + 2 * k] = col[k][0]
+            s_ref[slot + 2 * k + 1] = col[k][1]
+        for n, tile in enumerate(tiles):
+            s_ref[slot + 8 + 2 * n] = tile[g][0]
+            s_ref[slot + 9 + 2 * n] = tile[g][1]
 
         def entry(i, k):
-            return spread(2 + 2 * k, jj + i), spread(3 + 2 * k, jj + i)
-
-        d = [spread(2 + 2 * k, jj + k) for k in range(4)]
+            return spread(2 * k, jj + i), spread(2 * k + 1, jj + i)
+
+        d = [spread(2 * k, jj + k) for k in range(4)]
         a01, a02, a03 = entry(0, 1), entry(0, 2), entry(0, 3)
         a12, a13, a23 = entry(1, 2), entry(1, 3), entry(2, 3)
         t1 = 1.0 / (d[0] * d[1] - (a01[0] * a01[0] + a01[1] * a01[1]))
@@ -83,73 +87,67 @@
         s11 = d[3] - (cjmul(a03, w01)[0] + cjmul(a13, w11)[0])
         s01 = dif(a23, add(cjmul(a02, w01), cjmul(a12, w11)))
         t2 = 1.0 / (s00 * s11 - (s01[0] * s01[0] + s01[1] * s01[1]))
-        m0 = scale(t1, dif(scale(d[1], p[0]), cmul(a01, p[1])))
-        m1 = scale(t1, dif(scale(d[0], p[1]), cjmul(a01, p[0])))
-        q2 = dif(p[2], add(cjmul(a02, m0), cjmul(a12, m1)))
-        q3 = dif(p[3], add(cjmul(a03, m0), cjmul(a13, m1)))
-        n2 = scale(t2, dif(scale(s11, q2), cmul(s01, q3)))
-        n3 = scale(t2, dif(scale(s00, q3), cjmul(s01, q2)))
-        n0 = dif(m0, add(cmul(w00, n2), cmul(w01, n3)))
-        n1 = dif(m1, add(cmul(w10, n2), cmul(w11, n3)))
-        new = [n0, n1, n2, n3]
-        br, bi = [], []
+        news = []
+        for n in range(len(tiles)):
+            p = [(spread(8 + 2 * n, jj + i), spread(9 + 2 * n, jj + i)) for i in range(4)]
+            m0 = scale(t1, dif(scale(d[1], p[0]), cmul(a01, p[1])))
+            m1 = scale(t1, dif(scale(d[0], p[1]), cjmul(a01, p[0])))
+            q2 = dif(p[2], add(cjmul(a02, m0), cjmul(a12, m1)))
+            q3 = dif(p[3], add(cjmul(a03, m0), cjmul(a13, m1)))
+            n2 = scale(t2, dif(scale(s11, q2), cmul(s01, q3)))
+            n3 = scale(t2, dif(scale(s00, q3), cjmul(s01, q2)))
+            n0 = dif(m0, add(cmul(w00, n2), cmul(w01, n3)))
+            n1 = dif(m1, add(cmul(w10, n2), cmul(w11, n3)))
+            news.append([n0, n1, n2, n3])
+        after = [[] for _ in tiles]
         for h in range(NB // 8):
-            c = col if h == g else [(lane(ar[h], at + k), lane(ai[h], at + k)) for k in range(4)]
-            u = add(add(cmul(c[0], n0), cmul(c[1], n1)), add(cmul(c[2], n2), cmul(c[3], n3)))
-            ur, ui = ar[h] - u[0], ai[h] - u[1]
-            if h == g:
-                for i in range(4):
-                    ur = jnp.where(row == jj + i, new[i][0], ur)
-                    ui = jnp.where(row == jj + i, new[i][1], ui)
-            br.append(ur)
-            bi.append(ui)
-        ar, ai = br, bi
-    return ar, ai
-
-
-def times_i(x, n):
-    tail = x[:, 2 * n :]
-    lane_no = lax.broadcasted_iota(jnp.int32, tail.shape, 1)
-    back, fwd = pltpu.roll(tail, LANES - 1, 1), pltpu.roll(tail, 1, 1)
-    return jnp.concatenate([-x[:, n : 2 * n], x[:, :n], jnp.where(lane_no == 0, -back, fwd)], 1)
+            c = col if h == g else column(h)
+            for n, tile in enumerate(tiles):
+                new = news[n]
+                u = add(
+                    add(cmul(c[0], new[0]), cmul(c[1], new[1])), add(cmul(c[2], new[2]), cmul(c[3], new[3]))
+                )
+                ur, ui = dif(tile[h], u)
+                if h == g:
+                    for i in range(4):
+                        ur = jnp.where(row == jj + i, new[i][0], ur)
+                        ui = jnp.where(row == jj + i, new[i][1], ui)
+                after[n].append((ur, ui))
+        tiles = after
+    return [[jnp.concatenate([piece[part] for piece in tile], 0) for part in range(2)] for tile in tiles]
+
+
+def turned(re, im):
+    return jnp.concatenate([jnp.concatenate([re, im], 1), jnp.concatenate([-im, re], 1)], 0)
 
 
 def solve_in(w_ref, s_ref):
-    lanes = lax.broadcasted_iota(jnp.int32, (8, LANES), 1)
-    rows = lax.broadcasted_iota(jnp.int32, (8, LANES), 0)
-    dr, di = w_ref[:NB, :LANES], w_ref[:NB, CH : CH + LANES]
+    parts = [(w_ref[:NB, o : o + LANES], w_ref[:NB, PART + o : PART + o + LANES]) for o in range(0, PART, LANES)]
+    per_tile = LANES // NB
     for k in range(CH // NB):
-        t, u = divmod(k, LANES // NB)
-        base, other = NB * u, NB * ((u + 1) % (LANES // NB))
-        inside = (lanes >= base) & (lanes < base + NB)
-        ar, ai = [], []
-        for h in range(NB // 8):
-            unit = jnp.where(lanes == other + 8 * h + rows, 1.0, 0.0)
-            ar.append(jnp.where(inside, dr[8 * h : 8 * h + 8], unit))
-            ai.append(jnp.where(inside, di[8 * h : 8 * h + 8], 0.0))
-        ar, ai = gauss_jordan(ar, ai, base, s_ref)
-        ar, ai = jnp.concatenate(ar, 0), jnp.concatenate(ai, 0)
-        inv = jnp.concatenate([ar[:, other : other + NB], ai[:, other : other + NB]], 1)
-        mine = slice(NB * k, NB * k + NB)
-        live = slice(LANES * t, CH), slice(CH + LANES * t, 2 * CH), slice(2 * CH, 2 * CH + LANES)
-        n = CH - LANES * t
-        x = jnp.concatenate([w_ref[mine, s] for s in live], 1)
-        y = dot(inv, jnp.concatenate([x, times_i(x, n)], 0))
-        yy = jnp.concatenate([y, times_i(y, n)], 0)
-        at = LANES * t + base
-        c = jnp.concatenate([w_ref[:, at : at + NB], w_ref[:, CH + at : CH + at + NB]], 1)
+        t, u = divmod(k, per_tile)
+        mine, nxt = slice(NB * k, NB * k + NB), slice(NB * k + NB, NB * k + 2 * NB)
+        tiles = [[(a[8 * h : 8 * h + 8], b[8 * h : 8 * h + 8]) for h in range(NB // 8)] for a, b in parts]
+        tiles = gauss_jordan(tiles, NB * u, s_ref)
+        re, im = (jnp.concatenate([tile[part] for tile in tiles], 1) for part in range(2))
+        both = turned(re, im)
+        n = PART - LANES * t
+        at = LANES * t + NB * u
+        c = jnp.concatenate([w_ref[:, at : at + NB], w_ref[:, PART + at : PART + at + NB]], 1)
         if k + 1 < CH // NB:
-            nxt = slice(NB * k + NB, NB * k + 2 * NB)
-            o = LANES * ((k + 1) // (LANES // NB) - t)
-            e = LANES * t + o
-            both = jnp.concatenate([yy[:, o : o + LANES], yy[:, n + o : n + o + LANES]], 1)
             step = dot(c[nxt], both)
-            dr = w_ref[nxt, e : e + LANES] - step[:, :LANES]
-            di = w_ref[nxt, CH + e : CH + e + LANES] - step[:, LANES:]
-        upd = dot(c, yy)
-        for s, o, m in zip(live, (0, n, 2 * n), (n, n, LANES)):
-            w_ref[:, s] = w_ref[:, s] - upd[:, o : o + m]
-            w_ref[mine, s] = y[:, o : o + m]
+            first = LANES * ((k + 1) // per_tile)
+            parts = [
+                (
+                    w_ref[nxt, o : o + LANES] - step[:, o - LANES * t : o - LANES * t + LANES],
+                    w_ref[nxt, PART + o : PART + o + LANES] - step[:, n + o - LANES * t : n + o - LANES * t + LANES],
+                )
+                for o in range(first, PART, LANES)
+            ]
+        upd = dot(c, both)
+        for s, o, y in ((slice(LANES * t, PART), 0, re), (slice(PART + LANES * t, 2 * PART), n, im)):
+            w_ref[:, s] = w_ref[:, s] - upd[:, o : o + n]
+            w_ref[mine, s] = y
 
 
 def cells_of(x_ref, s):
@@ -185,15 +183,16 @@
     diag = lax.broadcasted_iota(jnp.int32, (CH, CH), 0) == lax.broadcasted_iota(jnp.int32, (CH, CH), 1)
     loading = 0.1 * jnp.sum(jnp.where(diag, re, 0.0), keepdims=True) / CH + 1e-5
     w_ref[:, :CH] = re + jnp.where(diag, loading, 0.0)
-    w_ref[:, CH : 2 * CH] = im
-    w_ref[:, 2 * CH :] = rhs_ref[...]
+    w_ref[:, CH:PART] = rhs_ref[0]
+    w_ref[:, PART : PART + CH] = im
+    w_ref[:, PART + CH :] = rhs_ref[1]
     return loading
 
 
 def beams_out(x_ref, m_ref, w_ref, loading, out_ref):
-    wt = jnp.transpose(w_ref[:, 2 * CH :])[:8]
-    wt = wt.astype(jnp.bfloat16).astype(jnp.float32)
-    wr, wi = wt[0:1], wt[1:2]
+    wr, wi = (
+        jnp.transpose(w_ref[:, o : o + LANES])[:1].astype(jnp.bfloat16).astype(jnp.float32) for o in (CH, PART + CH)
+    )
     first = lax.broadcasted_iota(jnp.int32, (8, CH), 0)
     left = jnp.where(first == 0, wr, jnp.where(first == 1, -wi, 0.0))
     right = jnp.where(first == 0, wi, jnp.where(first == 1, wr, 0.0))
@@ -212,7 +211,7 @@
         return p
 
     p = lax.fori_loop(0, CELLS // LANES // UNROLL, step, jnp.zeros((8, LANES), jnp.float32))
-    sq = jnp.sum(jnp.where(first < 2, wt * wt, 0.0), keepdims=True)
+    sq = jnp.sum(wr * wr + wi * wi, keepdims=True)
     power = jnp.sum(p, keepdims=True) * (1.0 / CELLS) + loading * sq
     out_ref[...] = out_ref[...] * lax.rsqrt(power).reshape(1, 1, 1)
 
@@ -237,7 +236,7 @@
         out_specs=pl.BlockSpec(memory_space=pltpu.VMEM),
         scratch_shapes=[
             pltpu.VMEM(x.shape, x.dtype),
-            pltpu.VMEM((CH, 2 * CH + LANES), jnp.float32),
+            pltpu.VMEM((CH, 2 * PART), jnp.float32),
             pltpu.VMEM((2 * CH, CH), jnp.float32),
             pltpu.VMEM((2 * SLOTS, 8, LANES), jnp.float32),
             pltpu.SemaphoreType.DMA((CELLS // LANES // UNROLL,)),
@@ -267,7 +266,7 @@
     ).astype(ml_dtypes.bfloat16)
 
 
-PIECES = 4
+PIECES = 2
 
 
 def transform_kernel(
@@ -291,16 +290,16 @@
         )
 
     table_copy = pltpu.make_async_copy(table_hbm, table_ref, table_sem)
-    for g in range(groups):
-        for i in range(PIECES):
-            fetch(g, i).start()
-        if g == 0:
-            table_copy.start()
+    for i in range(PIECES):
+        fetch(0, i).start()
+    table_copy.start()
     flat = wide_ref.reshape(depth * IN_STRIDE, LANES)
     bflat = back_ref.reshape(bins * OUT_STRIDE, LANES)
     for g in range(groups):
         for i in range(PIECES):
             fetch(g, i).wait()
+            if g + 1 < groups:
+                fetch(g + 1, i).start()
             rows = pl.ds(step * i, step)
             wide_ref[rows, :GROUP] = raw_ref[g, rows].astype(jnp.float32)
         if g == 0:
@@ -353,8 +352,8 @@
 def steering(index, channels):
     sine_of = -0.9 + 1.8 * index.astype(jnp.float32) / (NANG - 1)
     phase_angle = math.pi * jnp.arange(channels, dtype=jnp.float32) * sine_of
-    pair = jnp.stack([jnp.cos(phase_angle), jnp.sin(phase_angle)], 1)
-    return jnp.pad(pair, ((0, 0), (0, LANES - 2)))
+    pair = jnp.stack([jnp.cos(phase_angle), jnp.sin(phase_angle)])
+    return jnp.pad(pair[:, :, None], ((0, 0), (0, 0), (0, LANES - 1)))
 
 
 def on_device(pulses, guard, steer_index):

time: 159 us -> 158 us (level)
  no operation moved by 1% of the time
where the time goes in v4:
time: 158 us
  waiting for transfers between devices  71.9 us (46%)
  blocking collectives  34.9 us (22%)
  Pallas kernels  31 us (20%)
  starting transfers between devices  16.7 us (11%)
  local copies, waits for them, and re-layouts  2.11 us (1%)
    all_to_all x1, waiting for transfers between devices, on_device(): lax.all_to_all(spectrum, ('rng', 'dop'), split_axis=0, concat_axis=0, til...  71.9 us
    all_gather x1, blocking collectives, on_device(): mask = 1.0 - lax.all_gather(guard, 'rng', axis=0).astype(jnp.float32)  22.7 us
    pallas_call x1, Pallas kernels, one_bin(): pl.pallas_call(bin_kernel, out_shape=jax.ShapeDtypeStruct((CELLS // LANES...  20.9 us
    all_to_all x1, starting transfers between devices, on_device(): lax.all_to_all(spectrum, ('rng', 'dop'), split_axis=0, concat_axis=0, til...  16.7 us
    all_to_all x1, blocking collectives, on_device(): return lax.all_to_all(beams, 'rng', split_axis=0, concat_axis=0, tiled=True)  12.2 us
    pallas_call x1, Pallas kernels, transform(): pl.pallas_call(transform_kernel, out_shape=jax.ShapeDtypeStruct((bins, 2,...  10.1 us
  transfers between devices with their start and end apart: 1, of which 1 were waited for; matrix products, arithmetic and copies ran while one was open for 1% of the time, Pallas kernels for 0%

profile of v4, /device:TPU:1, one launch (start us, length us, event | category | flops | bytes accessed | tf_op | source)
XLA Modules:
  0.0 158.0 jit_solution(7675097080865353503)
XLA Ops:
  0.0 10.1 %transform.1 = bf16[256,2,32,128]{3,2,1,0:T(8,128)(2,1)} custom-call(bf16[512,1024]{1,0:T(8,128)(2,1)} %constant.28.clone.table_hbm, bf16[2,512,32,128]{3,2,1,0:T(8,128)(2,1)} %x_hbm.1), custom_call_target="tpu_custom_call" | custom-call | tf_op jit(solution)/shard_map/transform/pallas_call | solution.py:327
  10.1 0.0 copy-start.1
  10.1 0.0 copy-start
  10.1 16.7 %all-to-all-start = ((bf16[256,2,32,128]{3,2,1,0:T(8,128)(2,1)}), bf16[256,2,32,128]{3,2,1,0:T(8,128)(2,1)}, u32[]{:S(2)}, u32[]{:S(2)}) async-start(bf16[256,2,32,128]{3,2,1,0:T(8,128)(2,1)} %transform.1), calls=%async_computation | async-start | bytes 8388608 | tf_op jit(solution)/shard_map/all_to_all | solution.py:364
  26.8 0.0 copy-done.1
  26.8 0.6 dynamic_slice.3
  28.1 0.1 fusion
  28.1 0.1 copy.9
  28.3 0.7 pad.4.rhs_ref
  29.0 0.0 copy-done
  29.0 22.7 %all-gather.1 = s32[32,1,128]{2,1,0:T(1,128)S(1)} all-gather(s32[1,1,128]{2,1,0:T(1,128)S(1)} %bitcast.9), channel_id=2, replica_groups=mesh['rng'=32,'dop'=8] {'rng'}, dimensions={0}, use_global_device_ids=true | all-gather | bytes 16896 | tf_op jit(solution)/shard_map/all_gather | solution.py:362
  51.8 0.6 subtract_bitcast_fusion.m_ref
  52.4 71.9 %all-to-all-done = bf16[256,2,32,128]{3,2,1,0:T(8,128)(2,1)} async-done(((bf16[256,2,32,128]{3,2,1,0:T(8,128)(2,1)}), bf16[256,2,32,128]{3,2,1,0:T(8,128)(2,1)}, u32[]{:S(2)}, u32[]{:S(2)}) %all-to-all-start) | async-done | bytes 4194336 | tf_op jit(solution)/shard_map/all_to_all | solution.py:364
  124.3 20.9 %one_bin.1 = f32[32,2,128]{2,1,0:T(2,128)} custom-call(bf16[32,8,64,128]{3,2,1,0:T(8,128)(2,1)} %bitcast.x_hbm, f32[32,128]{1,0:T(8,128)} %subtract_bitcast_fusion.m_ref, f32[2,256,128]{2,1,0:T(8,128)} %pad.4.rhs_ref), custom_call_target="tpu_custom_call" | custom-call | tf_op jit(solution)/shard_map/one_bin/pallas_call | solution.py:232
  145.2 12.2 %all_to_all.10 = f32[32,2,128]{2,1,0:T(2,128)S(1)} all-to-all(f32[32,2,128]{2,1,0:T(2,128)} %one_bin.1), channel_id=1, replica_groups=mesh['rng'=32,'dop'=8] {'rng'}, dimensions={0} | all-to-all | bytes 65536 | tf_op jit(solution)/shard_map/all_to_all | solution.py:366
  157.4 0.6 copy.11
  (1 shorter events, 0.0 us)
Async XLA Ops:
  10.1 16.7 %copy-start.1 = (s32[32]{0:T(128)S(1)}, s32[32]{0:T(128)}, u32[]{:S(2)}) copy-start(s32[32]{0:T(128)} %param.6) | copy-start | bytes 388
  10.1 18.9 %copy-start = (s32[128]{0:T(128)S(1)}, s32[128]{0:T(128)}, u32[]{:S(2)}) copy-start(s32[128]{0:T(128)} %param.5) | copy-start | bytes 1540
  10.1 114.2 %all-to-all-start = ((bf16[256,2,32,128]{3,2,1,0:T(8,128)(2,1)}), bf16[256,2,32,128]{3,2,1,0:T(8,128)(2,1)}, u32[]{:S(2)}, u32[]{:S(2)}) async-start(bf16[256,2,32,128]{3,2,1,0:T(8,128)(2,1)} %transform.1), calls=%async_computation | async-start | bytes 8388608 | tf_op jit(solution)/shard_map/all_to_all | solution.py:364

commit v5 on v4

--- a/solution.py
+++ b/solution.py
@@ -121,33 +121,52 @@
     return jnp.concatenate([jnp.concatenate([re, im], 1), jnp.concatenate([-im, re], 1)], 0)
 
 
+def live_tiles(k):
+    per_tile = LANES // NB
+    if k == 0:
+        return [0, LANES, CH]
+    if k < per_tile:
+        return [0, LANES]
+    return [LANES, 0] if k == per_tile else [LANES]
+
+
 def solve_in(w_ref, s_ref):
-    parts = [(w_ref[:NB, o : o + LANES], w_ref[:NB, PART + o : PART + o + LANES]) for o in range(0, PART, LANES)]
-    per_tile = LANES // NB
+    def block(rows, at):
+        return w_ref[rows, at : at + LANES], w_ref[rows, PART + at : PART + at + LANES]
+
+    parts = [block(slice(0, NB), at) for at in live_tiles(0)]
     for k in range(CH // NB):
-        t, u = divmod(k, per_tile)
         mine, nxt = slice(NB * k, NB * k + NB), slice(NB * k + NB, NB * k + 2 * NB)
+        live, then = live_tiles(k), live_tiles(min(k + 1, CH // NB - 1))
+        moved = (live[-1], then[0]) if len(then) < len(live) else None
         tiles = [[(a[8 * h : 8 * h + 8], b[8 * h : 8 * h + 8]) for h in range(NB // 8)] for a, b in parts]
-        tiles = gauss_jordan(tiles, NB * u, s_ref)
+        tiles = gauss_jordan(tiles, NB * k % LANES, s_ref)
         re, im = (jnp.concatenate([tile[part] for tile in tiles], 1) for part in range(2))
         both = turned(re, im)
-        n = PART - LANES * t
-        at = LANES * t + NB * u
-        c = jnp.concatenate([w_ref[:, at : at + NB], w_ref[:, PART + at : PART + at + NB]], 1)
+        n = LANES * len(live)
+        c = jnp.concatenate([w_ref[:, NB * k : NB * k + NB], w_ref[:, PART + NB * k : PART + NB * k + NB]], 1)
         if k + 1 < CH // NB:
             step = dot(c[nxt], both)
-            first = LANES * ((k + 1) // per_tile)
-            parts = [
-                (
-                    w_ref[nxt, o : o + LANES] - step[:, o - LANES * t : o - LANES * t + LANES],
-                    w_ref[nxt, PART + o : PART + o + LANES] - step[:, n + o - LANES * t : n + o - LANES * t + LANES],
-                )
-                for o in range(first, PART, LANES)
-            ]
+            fresh = {}
+            for i, at in enumerate(live):
+                a, b = block(nxt, at)
+                o = LANES * i
+                fresh[at] = a - step[:, o : o + LANES], b - step[:, n + o : n + o + LANES]
+            if moved:
+                lane0 = lax.broadcasted_iota(jnp.int32, (NB, LANES), 1) == 0
+                fresh[moved[1]] = tuple(jnp.where(lane0, a, b) for a, b in zip(fresh[moved[0]], fresh[moved[1]]))
+            parts = [fresh[at] for at in then]
         upd = dot(c, both)
-        for s, o, y in ((slice(LANES * t, PART), 0, re), (slice(PART + LANES * t, 2 * PART), n, im)):
-            w_ref[:, s] = w_ref[:, s] - upd[:, o : o + n]
-            w_ref[mine, s] = y
+        for i, at in enumerate(live):
+            for first, o, y in ((at, LANES * i, re), (PART + at, n + LANES * i, im)):
+                s = slice(first, first + LANES)
+                w_ref[:, s] = w_ref[:, s] - upd[:, o : o + LANES]
+                w_ref[mine, s] = y[:, LANES * i : LANES * i + LANES]
+        if moved:
+            lane0 = lax.broadcasted_iota(jnp.int32, (CH, LANES), 1) == 0
+            for first in (0, PART):
+                s, d = (slice(first + at, first + at + LANES) for at in moved)
+                w_ref[:, d] = jnp.where(lane0, w_ref[:, s], w_ref[:, d])
 
 
 def cells_of(x_ref, s):
@@ -191,7 +210,7 @@
 
 def beams_out(x_ref, m_ref, w_ref, loading, out_ref):
     wr, wi = (
-        jnp.transpose(w_ref[:, o : o + LANES])[:1].astype(jnp.bfloat16).astype(jnp.float32) for o in (CH, PART + CH)
+        jnp.transpose(w_ref[:, o : o + LANES])[:1].astype(jnp.bfloat16).astype(jnp.float32) for o in (LANES, PART + LANES)
     )
     first = lax.broadcasted_iota(jnp.int32, (8, CH), 0)
     left = jnp.where(first == 0, wr, jnp.where(first == 1, -wi, 0.0))

time: 158 us -> 157 us (level)
  no operation moved by 1% of the time
where the time goes in v5:
time: 157 us
  waiting for transfers between devices  71.9 us (46%)
  blocking collectives  34.9 us (22%)
  Pallas kernels  29.7 us (19%)
  starting transfers between devices  16.7 us (11%)
  local copies, waits for them, and re-layouts  2.11 us (1%)
    all_to_all x1, waiting for transfers between devices, on_device(): lax.all_to_all(spectrum, ('rng', 'dop'), split_axis=0, concat_axis=0, til...  71.9 us
    all_gather x1, blocking collectives, on_device(): mask = 1.0 - lax.all_gather(guard, 'rng', axis=0).astype(jnp.float32)  22.7 us
    pallas_call x1, Pallas kernels, one_bin(): pl.pallas_call(bin_kernel, out_shape=jax.ShapeDtypeStruct((CELLS // LANES...  19.6 us
    all_to_all x1, starting transfers between devices, on_device(): lax.all_to_all(spectrum, ('rng', 'dop'), split_axis=0, concat_axis=0, til...  16.7 us
    all_to_all x1, blocking collectives, on_device(): return lax.all_to_all(beams, 'rng', split_axis=0, concat_axis=0, tiled=True)  12.2 us
    pallas_call x1, Pallas kernels, transform(): pl.pallas_call(transform_kernel, out_shape=jax.ShapeDtypeStruct((bins, 2,...  10.1 us
  transfers between devices with their start and end apart: 1, of which 1 were waited for; matrix products, arithmetic and copies ran while one was open for 1% of the time, Pallas kernels for 0%

profile of v5, /device:TPU:1, one launch (start us, length us, event | category | flops | bytes accessed | tf_op | source)
XLA Modules:
  0.0 156.7 jit_solution(4661492155756718290)
XLA Ops:
  0.0 10.1 %transform.1 = bf16[256,2,32,128]{3,2,1,0:T(8,128)(2,1)} custom-call(bf16[512,1024]{1,0:T(8,128)(2,1)} %constant.28.clone.table_hbm, bf16[2,512,32,128]{3,2,1,0:T(8,128)(2,1)} %x_hbm.1), custom_call_target="tpu_custom_call" | custom-call | tf_op jit(solution)/shard_map/transform/pallas_call | solution.py:346
  10.1 0.0 copy-start.1
  10.1 0.0 copy-start
  10.1 16.7 %all-to-all-start = ((bf16[256,2,32,128]{3,2,1,0:T(8,128)(2,1)}), bf16[256,2,32,128]{3,2,1,0:T(8,128)(2,1)}, u32[]{:S(2)}, u32[]{:S(2)}) async-start(bf16[256,2,32,128]{3,2,1,0:T(8,128)(2,1)} %transform.1), calls=%async_computation | async-start | bytes 8388608 | tf_op jit(solution)/shard_map/all_to_all | solution.py:383
  26.8 0.0 copy-done.1
  26.8 0.6 dynamic_slice.3
  28.1 0.1 fusion
  28.1 0.1 copy.9
  28.3 0.7 pad.4.rhs_ref
  29.0 0.0 copy-done
  29.0 22.7 %all-gather.1 = s32[32,1,128]{2,1,0:T(1,128)S(1)} all-gather(s32[1,1,128]{2,1,0:T(1,128)S(1)} %bitcast.9), channel_id=2, replica_groups=mesh['rng'=32,'dop'=8] {'rng'}, dimensions={0}, use_global_device_ids=true | all-gather | bytes 16896 | tf_op jit(solution)/shard_map/all_gather | solution.py:381
  51.8 0.6 subtract_bitcast_fusion.m_ref
  52.4 71.9 %all-to-all-done = bf16[256,2,32,128]{3,2,1,0:T(8,128)(2,1)} async-done(((bf16[256,2,32,128]{3,2,1,0:T(8,128)(2,1)}), bf16[256,2,32,128]{3,2,1,0:T(8,128)(2,1)}, u32[]{:S(2)}, u32[]{:S(2)}) %all-to-all-start) | async-done | bytes 4194336 | tf_op jit(solution)/shard_map/all_to_all | solution.py:383
  124.3 19.6 %one_bin.1 = f32[32,2,128]{2,1,0:T(2,128)} custom-call(bf16[32,8,64,128]{3,2,1,0:T(8,128)(2,1)} %bitcast.x_hbm, f32[32,128]{1,0:T(8,128)} %subtract_bitcast_fusion.m_ref, f32[2,256,128]{2,1,0:T(8,128)} %pad.4.rhs_ref), custom_call_target="tpu_custom_call" | custom-call | tf_op jit(solution)/shard_map/one_bin/pallas_call | solution.py:251
  143.9 12.2 %all_to_all.10 = f32[32,2,128]{2,1,0:T(2,128)S(1)} all-to-all(f32[32,2,128]{2,1,0:T(2,128)} %one_bin.1), channel_id=1, replica_groups=mesh['rng'=32,'dop'=8] {'rng'}, dimensions={0} | all-to-all | bytes 65536 | tf_op jit(solution)/shard_map/all_to_all | solution.py:385
  156.1 0.6 copy.11
  (1 shorter events, 0.0 us)
Async XLA Ops:
  10.1 16.7 %copy-start.1 = (s32[32]{0:T(128)S(1)}, s32[32]{0:T(128)}, u32[]{:S(2)}) copy-start(s32[32]{0:T(128)} %param.6) | copy-start | bytes 388
  10.1 18.9 %copy-start = (s32[128]{0:T(128)S(1)}, s32[128]{0:T(128)}, u32[]{:S(2)}) copy-start(s32[128]{0:T(128)} %param.5) | copy-start | bytes 1540
  10.1 114.2 %all-to-all-start = ((bf16[256,2,32,128]{3,2,1,0:T(8,128)(2,1)}), bf16[256,2,32,128]{3,2,1,0:T(8,128)(2,1)}, u32[]{:S(2)}, u32[]{:S(2)}) async-start(bf16[256,2,32,128]{3,2,1,0:T(8,128)(2,1)} %transform.1), calls=%async_computation | async-start | bytes 8388608 | tf_op jit(solution)/shard_map/all_to_all | solution.py:383

commit v6 on v5

--- a/solution.py
+++ b/solution.py
@@ -64,7 +64,11 @@
         def column(h):
             return [(lane(tiles[0][h][0], at + k), lane(tiles[0][h][1], at + k)) for k in range(4)]
 
-        col = column(g)
+        if jj == 0:
+            col = column(g)
+            ahead = [tuple(lane(piece, at + 4 + k) for piece in tiles[0][g]) for k in range(4)]
+        else:
+            col = ahead
         for k in range(4):
             s_ref[slot + 2 * k] = col[k][0]
             s_ref[slot + 2 * k + 1] = col[k][1]
@@ -87,9 +91,8 @@
         s11 = d[3] - (cjmul(a03, w01)[0] + cjmul(a13, w11)[0])
         s01 = dif(a23, add(cjmul(a02, w01), cjmul(a12, w11)))
         t2 = 1.0 / (s00 * s11 - (s01[0] * s01[0] + s01[1] * s01[1]))
-        news = []
-        for n in range(len(tiles)):
-            p = [(spread(8 + 2 * n, jj + i), spread(9 + 2 * n, jj + i)) for i in range(4)]
+
+        def new_rows(p):
             m0 = scale(t1, dif(scale(d[1], p[0]), cmul(a01, p[1])))
             m1 = scale(t1, dif(scale(d[0], p[1]), cjmul(a01, p[0])))
             q2 = dif(p[2], add(cjmul(a02, m0), cjmul(a12, m1)))
@@ -98,21 +101,31 @@
             n3 = scale(t2, dif(scale(s00, q3), cjmul(s01, q2)))
             n0 = dif(m0, add(cmul(w00, n2), cmul(w01, n3)))
             n1 = dif(m1, add(cmul(w10, n2), cmul(w11, n3)))
-            news.append([n0, n1, n2, n3])
+            return [n0, n1, n2, n3]
+
+        def less(piece, c, new):
+            u = add(add(cmul(c[0], new[0]), cmul(c[1], new[1])), add(cmul(c[2], new[2]), cmul(c[3], new[3])))
+            return dif(piece, u)
+
+        def with_rows(piece, new):
+            for i in range(4):
+                piece = tuple(jnp.where(row == jj + i, new[i][part], piece[part]) for part in range(2))
+            return piece
+
+        if jj == 0:
+            turned_rows = new_rows([(c[0], -c[1]) for c in col])
+            for k in range(4):
+                new = [(sub(v[0], 4 + k), sub(v[1], 4 + k)) for v in turned_rows]
+                ahead[k] = with_rows(less(ahead[k], col, new), new)
+        news = []
+        for n in range(len(tiles)):
+            news.append(new_rows([(spread(8 + 2 * n, jj + i), spread(9 + 2 * n, jj + i)) for i in range(4)]))
         after = [[] for _ in tiles]
         for h in range(NB // 8):
             c = col if h == g else column(h)
             for n, tile in enumerate(tiles):
-                new = news[n]
-                u = add(
-                    add(cmul(c[0], new[0]), cmul(c[1], new[1])), add(cmul(c[2], new[2]), cmul(c[3], new[3]))
-                )
-                ur, ui = dif(tile[h], u)
-                if h == g:
-                    for i in range(4):
-                        ur = jnp.where(row == jj + i, new[i][0], ur)
-                        ui = jnp.where(row == jj + i, new[i][1], ui)
-                after[n].append((ur, ui))
+                piece = less(tile[h], c, news[n])
+                after[n].append(with_rows(piece, news[n]) if h == g else piece)
         tiles = after
     return [[jnp.concatenate([piece[part] for piece in tile], 0) for part in range(2)] for tile in tiles]
 
@@ -174,7 +187,7 @@
     return x[:, :32].reshape(CH, LANES), x[:, 32:].reshape(CH, LANES)
 
 
-UNROLL = 8
+UNROLL = 16
 
 
 def cov_in(x_ref, m_ref, rhs_ref, w_ref, acc_ref, arrive):
@@ -312,8 +325,8 @@
     for i in range(PIECES):
         fetch(0, i).start()
     table_copy.start()
-    flat = wide_ref.reshape(depth * IN_STRIDE, LANES)
-    bflat = back_ref.reshape(bins * OUT_STRIDE, LANES)
+    flat = wide_ref.reshape((depth + 1) * IN_STRIDE, LANES)
+    bflat = back_ref.reshape((bins + 1) * OUT_STRIDE, LANES)
     for g in range(groups):
         for i in range(PIECES):
             fetch(g, i).wait()
@@ -332,7 +345,7 @@
                         bins * k : bins * k + bins, LANES * i : LANES * i + LANES
                     ]
         for k in range(2):
-            out_ref[g, k] = back_ref[:, k * GROUP : k * GROUP + GROUP].astype(jnp.bfloat16)
+            out_ref[g, k] = back_ref[:bins, k * GROUP : k * GROUP + GROUP].astype(jnp.bfloat16)
             send(g, k).start()
     for g in range(groups):
         for k in range(2):
@@ -351,8 +364,8 @@
         scratch_shapes=[
             pltpu.VMEM((2 * bins, depth), jnp.bfloat16),
             pltpu.VMEM((groups, depth, GROUP, cells), jnp.bfloat16),
-            pltpu.VMEM((depth, IN_STRIDE, cells), jnp.float32),
-            pltpu.VMEM((bins, OUT_STRIDE, cells), jnp.float32),
+            pltpu.VMEM((depth + 1, IN_STRIDE, cells), jnp.float32),
+            pltpu.VMEM((bins + 1, OUT_STRIDE, cells), jnp.float32),
             pltpu.VMEM((groups, 2, bins, GROUP, cells), jnp.bfloat16),
             pltpu.SemaphoreType.DMA,
             pltpu.SemaphoreType.DMA((groups, PIECES)),

time: 157 us -> 156 us (level)
  no operation moved by 1% of the time
where the time goes in v6:
time: 156 us; the launch traced here: 155 us
  waiting for transfers between devices  71.9 us (46%)
  blocking collectives  35 us (22%)
  Pallas kernels  28.3 us (18%)
  starting transfers between devices  16.7 us (11%)
  local copies, waits for them, and re-layouts  2.11 us (1%)
    all_to_all x1, waiting for transfers between devices, on_device(): lax.all_to_all(spectrum, ('rng', 'dop'), split_axis=0, concat_axis=0, til...  71.9 us
    all_gather x1, blocking collectives, on_device(): mask = 1.0 - lax.all_gather(guard, 'rng', axis=0).astype(jnp.float32)  22.7 us
    pallas_call x1, Pallas kernels, one_bin(): pl.pallas_call(bin_kernel, out_shape=jax.ShapeDtypeStruct((CELLS // LANES...  18.2 us
    all_to_all x1, starting transfers between devices, on_device(): lax.all_to_all(spectrum, ('rng', 'dop'), split_axis=0, concat_axis=0, til...  16.7 us
    all_to_all x1, blocking collectives, on_device(): return lax.all_to_all(beams, 'rng', split_axis=0, concat_axis=0, tiled=True)  12.2 us
    pallas_call x1, Pallas kernels, transform(): pl.pallas_call(transform_kernel, out_shape=jax.ShapeDtypeStruct((bins, 2,...  10.1 us
  transfers between devices with their start and end apart: 1, of which 1 were waited for; matrix products, arithmetic and copies ran while one was open for 1% of the time, Pallas kernels for 0%

profile of v6, /device:TPU:1, one launch (start us, length us, event | category | flops | bytes accessed | tf_op | source)
XLA Modules:
  0.0 155.3 jit_solution(6152192604756608893)
XLA Ops:
  0.0 10.1 %transform.1 = bf16[256,2,32,128]{3,2,1,0:T(8,128)(2,1)} custom-call(bf16[512,1024]{1,0:T(8,128)(2,1)} %constant.28.clone.table_hbm, bf16[2,512,32,128]{3,2,1,0:T(8,128)(2,1)} %x_hbm.1), custom_call_target="tpu_custom_call" | custom-call | tf_op jit(solution)/shard_map/transform/pallas_call | solution.py:359
  10.1 0.0 copy-start.1
  10.1 0.0 copy-start
  10.1 16.7 %all-to-all-start = ((bf16[256,2,32,128]{3,2,1,0:T(8,128)(2,1)}), bf16[256,2,32,128]{3,2,1,0:T(8,128)(2,1)}, u32[]{:S(2)}, u32[]{:S(2)}) async-start(bf16[256,2,32,128]{3,2,1,0:T(8,128)(2,1)} %transform.1), calls=%async_computation | async-start | bytes 8388608 | tf_op jit(solution)/shard_map/all_to_all | solution.py:396
  26.8 0.0 copy-done.1
  26.8 0.6 dynamic_slice.3
  28.1 0.1 fusion
  28.1 0.1 copy.9
  28.3 0.7 pad.4.rhs_ref
  29.0 0.0 copy-done
  29.0 22.7 %all-gather.1 = s32[32,1,128]{2,1,0:T(1,128)S(1)} all-gather(s32[1,1,128]{2,1,0:T(1,128)S(1)} %bitcast.9), channel_id=2, replica_groups=mesh['rng'=32,'dop'=8] {'rng'}, dimensions={0}, use_global_device_ids=true | all-gather | bytes 16896 | tf_op jit(solution)/shard_map/all_gather | solution.py:394
  51.8 0.6 subtract_bitcast_fusion.m_ref
  52.4 71.9 %all-to-all-done = bf16[256,2,32,128]{3,2,1,0:T(8,128)(2,1)} async-done(((bf16[256,2,32,128]{3,2,1,0:T(8,128)(2,1)}), bf16[256,2,32,128]{3,2,1,0:T(8,128)(2,1)}, u32[]{:S(2)}, u32[]{:S(2)}) %all-to-all-start) | async-done | bytes 4194336 | tf_op jit(solution)/shard_map/all_to_all | solution.py:396
  124.3 18.2 %one_bin.1 = f32[32,2,128]{2,1,0:T(2,128)} custom-call(bf16[32,8,64,128]{3,2,1,0:T(8,128)(2,1)} %bitcast.x_hbm, f32[32,128]{1,0:T(8,128)} %subtract_bitcast_fusion.m_ref, f32[2,256,128]{2,1,0:T(8,128)} %pad.4.rhs_ref), custom_call_target="tpu_custom_call" | custom-call | tf_op jit(solution)/shard_map/one_bin/pallas_call | solution.py:264
  142.5 12.2 %all_to_all.10 = f32[32,2,128]{2,1,0:T(2,128)S(1)} all-to-all(f32[32,2,128]{2,1,0:T(2,128)} %one_bin.1), channel_id=1, replica_groups=mesh['rng'=32,'dop'=8] {'rng'}, dimensions={0} | all-to-all | bytes 65536 | tf_op jit(solution)/shard_map/all_to_all | solution.py:398
  154.7 0.6 copy.11
  (1 shorter events, 0.0 us)
Async XLA Ops:
  10.1 16.7 %copy-start.1 = (s32[32]{0:T(128)S(1)}, s32[32]{0:T(128)}, u32[]{:S(2)}) copy-start(s32[32]{0:T(128)} %param.6) | copy-start | bytes 388
  10.1 18.9 %copy-start = (s32[128]{0:T(128)S(1)}, s32[128]{0:T(128)}, u32[]{:S(2)}) copy-start(s32[128]{0:T(128)} %param.5) | copy-start | bytes 1540
  10.1 114.2 %all-to-all-start = ((bf16[256,2,32,128]{3,2,1,0:T(8,128)(2,1)}), bf16[256,2,32,128]{3,2,1,0:T(8,128)(2,1)}, u32[]{:S(2)}, u32[]{:S(2)}) async-start(bf16[256,2,32,128]{3,2,1,0:T(8,128)(2,1)} %transform.1), calls=%async_computation | async-start | bytes 8388608 | tf_op jit(solution)/shard_map/all_to_all | solution.py:396

commit v7 on v6

--- a/solution.py
+++ b/solution.py
@@ -201,17 +201,18 @@
             xr, xi = cells_of(x_ref, s)
             m = jnp.broadcast_to(m_ref[pl.ds(s, 1), :].astype(jnp.bfloat16), (CH, LANES))
             xr, xi = xr * m, xi * m
-            a += [xr, xi]
-            b += [xi, -xr]
+            a.append(xr)
+            b.append(xi)
         a, b = jnp.concatenate(a, 1), jnp.concatenate(b, 1)
-        acc_ref[...] += lax.dot_general(
-            jnp.concatenate([a, b], 0), a, (((1,), (1,)), ((), ())), preferred_element_type=jnp.float32
-        )
+        both = jnp.concatenate([a, b], 1)
+        across = (((1,), (1,)), ((), ()))
+        acc_ref[:CH] += lax.dot_general(both, both, across, preferred_element_type=jnp.float32)
+        acc_ref[CH:] += lax.dot_general(b, a, across, preferred_element_type=jnp.float32)
         return 0
 
     lax.fori_loop(0, CELLS // LANES // UNROLL, step, 0)
     re = acc_ref[:CH] * (1.0 / CELLS)
-    im = acc_ref[CH:] * (1.0 / CELLS)
+    im = (acc_ref[CH:] - jnp.transpose(acc_ref[CH:])) * (1.0 / CELLS)
     diag = lax.broadcasted_iota(jnp.int32, (CH, CH), 0) == lax.broadcasted_iota(jnp.int32, (CH, CH), 1)
     loading = 0.1 * jnp.sum(jnp.where(diag, re, 0.0), keepdims=True) / CH + 1e-5
     w_ref[:, :CH] = re + jnp.where(diag, loading, 0.0)

time: 156 us -> 155 us (level)
  no operation moved by 1% of the time
where the time goes in v7:
time: 155 us
  waiting for transfers between devices  71.9 us (46%)
  blocking collectives  34.9 us (23%)
  Pallas kernels  27.8 us (18%)
  starting transfers between devices  16.7 us (11%)
  local copies, waits for them, and re-layouts  2.11 us (1%)
    all_to_all x1, waiting for transfers between devices, on_device(): lax.all_to_all(spectrum, ('rng', 'dop'), split_axis=0, concat_axis=0, til...  71.9 us
    all_gather x1, blocking collectives, on_device(): mask = 1.0 - lax.all_gather(guard, 'rng', axis=0).astype(jnp.float32)  22.7 us
    pallas_call x1, Pallas kernels, one_bin(): pl.pallas_call(bin_kernel, out_shape=jax.ShapeDtypeStruct((CELLS // LANES...  17.7 us
    all_to_all x1, starting transfers between devices, on_device(): lax.all_to_all(spectrum, ('rng', 'dop'), split_axis=0, concat_axis=0, til...  16.7 us
    all_to_all x1, blocking collectives, on_device(): return lax.all_to_all(beams, 'rng', split_axis=0, concat_axis=0, tiled=True)  12.2 us
    pallas_call x1, Pallas kernels, transform(): pl.pallas_call(transform_kernel, out_shape=jax.ShapeDtypeStruct((bins, 2,...  10.1 us
  transfers between devices with their start and end apart: 1, of which 1 were waited for; matrix products, arithmetic and copies ran while one was open for 1% of the time, Pallas kernels for 0%

profile of v7, /device:TPU:1, one launch (start us, length us, event | category | flops | bytes accessed | tf_op | source)
XLA Modules:
  0.0 154.9 jit_solution(11533647264339892624)
XLA Ops:
  0.0 10.1 %transform.1 = bf16[256,2,32,128]{3,2,1,0:T(8,128)(2,1)} custom-call(bf16[512,1024]{1,0:T(8,128)(2,1)} %constant.28.clone.table_hbm, bf16[2,512,32,128]{3,2,1,0:T(8,128)(2,1)} %x_hbm.1), custom_call_target="tpu_custom_call" | custom-call | tf_op jit(solution)/shard_map/transform/pallas_call | solution.py:360
  10.1 0.0 copy-start.1
  10.1 0.0 copy-start
  10.1 16.7 %all-to-all-start = ((bf16[256,2,32,128]{3,2,1,0:T(8,128)(2,1)}), bf16[256,2,32,128]{3,2,1,0:T(8,128)(2,1)}, u32[]{:S(2)}, u32[]{:S(2)}) async-start(bf16[256,2,32,128]{3,2,1,0:T(8,128)(2,1)} %transform.1), calls=%async_computation | async-start | bytes 8388608 | tf_op jit(solution)/shard_map/all_to_all | solution.py:397
  26.8 0.0 copy-done.1
  26.8 0.6 dynamic_slice.3
  28.1 0.1 fusion
  28.1 0.1 copy.9
  28.3 0.7 pad.4.rhs_ref
  29.0 0.0 copy-done
  29.0 22.7 %all-gather.1 = s32[32,1,128]{2,1,0:T(1,128)S(1)} all-gather(s32[1,1,128]{2,1,0:T(1,128)S(1)} %bitcast.9), channel_id=2, replica_groups=mesh['rng'=32,'dop'=8] {'rng'}, dimensions={0}, use_global_device_ids=true | all-gather | bytes 16896 | tf_op jit(solution)/shard_map/all_gather | solution.py:395
  51.8 0.6 subtract_bitcast_fusion.m_ref
  52.4 71.9 %all-to-all-done = bf16[256,2,32,128]{3,2,1,0:T(8,128)(2,1)} async-done(((bf16[256,2,32,128]{3,2,1,0:T(8,128)(2,1)}), bf16[256,2,32,128]{3,2,1,0:T(8,128)(2,1)}, u32[]{:S(2)}, u32[]{:S(2)}) %all-to-all-start) | async-done | bytes 4194336 | tf_op jit(solution)/shard_map/all_to_all | solution.py:397
  124.3 17.7 %one_bin.1 = f32[32,2,128]{2,1,0:T(2,128)} custom-call(bf16[32,8,64,128]{3,2,1,0:T(8,128)(2,1)} %bitcast.x_hbm, f32[32,128]{1,0:T(8,128)} %subtract_bitcast_fusion.m_ref, f32[2,256,128]{2,1,0:T(8,128)} %pad.4.rhs_ref), custom_call_target="tpu_custom_call" | custom-call | tf_op jit(solution)/shard_map/one_bin/pallas_call | solution.py:265
  142.0 12.2 %all_to_all.10 = f32[32,2,128]{2,1,0:T(2,128)S(1)} all-to-all(f32[32,2,128]{2,1,0:T(2,128)} %one_bin.1), channel_id=1, replica_groups=mesh['rng'=32,'dop'=8] {'rng'}, dimensions={0} | all-to-all | bytes 65536 | tf_op jit(solution)/shard_map/all_to_all | solution.py:399
  154.2 0.6 copy.11
  (1 shorter events, 0.0 us)
Async XLA Ops:
  10.1 16.7 %copy-start.1 = (s32[32]{0:T(128)S(1)}, s32[32]{0:T(128)}, u32[]{:S(2)}) copy-start(s32[32]{0:T(128)} %param.6) | copy-start | bytes 388
  10.1 18.9 %copy-start = (s32[128]{0:T(128)S(1)}, s32[128]{0:T(128)}, u32[]{:S(2)}) copy-start(s32[128]{0:T(128)} %param.5) | copy-start | bytes 1540
  10.1 114.2 %all-to-all-start = ((bf16[256,2,32,128]{3,2,1,0:T(8,128)(2,1)}), bf16[256,2,32,128]{3,2,1,0:T(8,128)(2,1)}, u32[]{:S(2)}, u32[]{:S(2)}) async-start(bf16[256,2,32,128]{3,2,1,0:T(8,128)(2,1)} %transform.1), calls=%async_computation | async-start | bytes 8388608 | tf_op jit(solution)/shard_map/all_to_all | solution.py:397
